TPU v7x, 32 devices: a whole 2x2x4 slice. The times are simulated.
32 devices in a mesh: segment: 2 (over x), dp: 16 (over z, y, core).
Axes of the slice: x: 2, y: 2, z: 4, core: 2. Of those that a mesh axis runs over, the one named last changes fastest.
Arguments:
- patches: bfloat16 [32, 1024, 768], P(('segment', 'dp')), may hold values from -6 to 6
- lengths: int32 [32], replicated, may hold values from 576 to 1024, as said below
- keep_order: int32 [32, 1024], replicated, may hold values from 0 to 1023, as said below
- e_vectors: float32 [8, 768], P(None, ('segment', 'dp')), may hold values from -1.75 to 1.75
- e_qkv: float32 [768, 2304], P(('segment', 'dp')), may hold values from -0.21875 to 0.21875
- e_proj: float32 [768, 768], P(('segment', 'dp')), may hold values from -1.75 to 1.75
- e_fc1: float32 [768, 3072], P(('segment', 'dp')), may hold values from -0.21875 to 0.21875
- e_fc1_bias: float32 [3072], P(('segment', 'dp')), may hold values from -1.75 to 1.75
- e_fc2: float32 [3072, 768], P(('segment', 'dp')), may hold values from -0.109375 to 0.109375
- embed: float32 [768, 512], P(('segment', 'dp')), may hold values from -0.21875 to 0.21875
- d_vectors: float32 [10, 512], P(None, ('segment', 'dp')), may hold values from -1.75 to 1.75
- dec_pos: float32 [1024, 512], P(None, ('segment', 'dp')), may hold values from -6 to 6
- d_qkv: float32 [512, 1536], P(('segment', 'dp')), may hold values from -0.25 to 0.25
- d_proj: float32 [512, 512], P(('segment', 'dp')), may hold values from -6 to 6
- d_fc1: float32 [512, 2048], P(('segment', 'dp')), may hold values from -0.25 to 0.25
- d_fc1_bias: float32 [2048], P(('segment', 'dp')), may hold values from -1.75 to 1.75
- d_fc2: float32 [2048, 512], P(('segment', 'dp')), may hold values from -0.125 to 0.125
- cotangent: bfloat16 [32, 1024, 512], P(('segment', 'dp')), may hold values from -12 to 12
Outputs:
- decoded: bfloat16 [32, 1024, 512], P(('segment', 'dp'))
- patches_grad: float32 [32, 1024, 768], P(('segment', 'dp'))
- e_vectors_grad: float32 [8, 768], P(None, ('segment', 'dp'))
- e_qkv_grad: float32 [768, 2304], P(('segment', 'dp'))
- e_proj_grad: float32 [768, 768], P(('segment', 'dp'))
- e_fc1_grad: float32 [768, 3072], P(('segment', 'dp'))
- e_fc1_bias_grad: float32 [3072], P(('segment', 'dp'))
- e_fc2_grad: float32 [3072, 768], P(('segment', 'dp'))
- embed_grad: float32 [768, 512], P(('segment', 'dp'))
- d_vectors_grad: float32 [10, 512], P(None, ('segment', 'dp'))
- dec_pos_grad: float32 [1024, 512], P(None, ('segment', 'dp'))
- d_qkv_grad: float32 [512, 1536], P(('segment', 'dp'))
- d_proj_grad: float32 [512, 512], P(('segment', 'dp'))
- d_fc1_grad: float32 [512, 2048], P(('segment', 'dp'))
- d_fc1_bias_grad: float32 [2048], P(('segment', 'dp'))
- d_fc2_grad: float32 [2048, 512], P(('segment', 'dp'))
Inputs may be any that keep to these rules, and one draw needn't show every extreme that they name: Each cube holds either 576 or 1024 tokens; both lengths occur. `keep_order`: for a cube of n tokens the first n entries are a permutation of 0 to n - 1 and the others are n to 1023 in order; the visible tokens are the first n // 10 entries.
All inputs are finite; a program needn't handle non-finite values.
Results may differ from a plain program's by a relative error of at most 0.017.
Values may be sent and summed in bfloat16 or wider, within the bound.
A program may use at most 384 MiB of HBM per device.

v0:
```python
import jax
import jax.numpy as jnp
from jax import lax
from jax.sharding import PartitionSpec as P

HEADS_E = 12
HEADS_D = 16
VIS = 104


norm_eps = 1e-06
far_below = -1e30


def shifted(value, axis, steps):
    count = lax.axis_size(axis)
    first, last = (max(0, -steps), min(count, count - steps))
    return lax.ppermute(value, axis, [(source, source + steps) for source in range(first, last)])


def norm_rows(values, gain, shift):
    center = values - jnp.mean(values, axis=-1, keepdims=True)
    spread = jnp.mean(center * center, axis=-1, keepdims=True)
    return center * lax.rsqrt(spread + norm_eps) * (1.0 + gain) + shift


def exact_gelu(values):
    return jax.nn.gelu(values, approximate=False)


def split_heads(matrix, heads):
    return matrix.reshape(matrix.shape[0], heads, matrix.shape[1] // heads)


def attend_forward(queries, key_rows, value_rows, live, heads):
    total_rows, width = queries.shape
    block_rows = min(512, total_rows)
    scale = (width // heads) ** (-0.5)
    q_heads = split_heads(queries, heads)
    k_heads = split_heads(key_rows, heads)
    v_heads = split_heads(value_rows, heads)
    starts = jnp.arange(total_rows // block_rows, dtype=jnp.int32) * block_rows

    def one_block(start):
        q_block = lax.dynamic_slice_in_dim(q_heads, start, block_rows, 0)
        scores = (
            jnp.einsum("qhd,khd->hqk", q_block, k_heads, preferred_element_type=jnp.float32) * scale
        )
        scores = jnp.where(live[None, None, :], scores, far_below)
        highest = jnp.max(scores, axis=-1, keepdims=True)
        raised = jnp.exp(scores - highest)
        totals = jnp.sum(raised, axis=-1, keepdims=True)
        probs = (raised / totals).astype(jnp.bfloat16)
        mixed = jnp.einsum("hqk,khd->qhd", probs, v_heads, preferred_element_type=jnp.float32)
        return (mixed, (highest + jnp.log(totals))[..., 0])

    mixed, sums_log = lax.map(one_block, starts)
    return (mixed.reshape(total_rows, width), sums_log)


def attend_backward(queries, key_rows, value_rows, sums_log, grad_rows, live, heads):
    total_rows, width = queries.shape
    block_rows = min(512, total_rows)
    scale = (width // heads) ** (-0.5)
    q_heads = split_heads(queries, heads)
    k_heads = split_heads(key_rows, heads)
    v_heads = split_heads(value_rows, heads)
    g_heads = split_heads(grad_rows, heads)
    starts = jnp.arange(total_rows // block_rows, dtype=jnp.int32) * block_rows

    def one_block(carry, inputs):
        grad_keys, grad_values = carry
        start, block_log = inputs
        q_block = lax.dynamic_slice_in_dim(q_heads, start, block_rows, 0)
        g_block = lax.dynamic_slice_in_dim(g_heads, start, block_rows, 0)
        scores = (
            jnp.einsum("qhd,khd->hqk", q_block, k_heads, preferred_element_type=jnp.float32) * scale
        )
        scores = jnp.where(live[None, None, :], scores, far_below)
        probs = jnp.exp(scores - block_log[..., None])
        grad_values = grad_values + jnp.einsum(
            "hqk,qhd->khd", probs.astype(jnp.bfloat16), g_block, preferred_element_type=jnp.float32
        )
        grad_probs = jnp.einsum(
            "qhd,khd->hqk", g_block, v_heads, preferred_element_type=jnp.float32
        )
        inner = jnp.sum(grad_probs * probs, axis=-1, keepdims=True)
        grad_scores = (probs * (grad_probs - inner)).astype(jnp.bfloat16)
        grad_query = (
            jnp.einsum("hqk,khd->qhd", grad_scores, k_heads, preferred_element_type=jnp.float32)
            * scale
        )
        grad_keys = (
            grad_keys
            + jnp.einsum("hqk,qhd->khd", grad_scores, q_block, preferred_element_type=jnp.float32)
            * scale
        )
        return ((grad_keys, grad_values), grad_query)

    empty = jnp.zeros(k_heads.shape, jnp.float32)
    (grad_keys, grad_values), grad_query = lax.scan(one_block, (empty, empty), (starts, sums_log))
    return (
        grad_query.reshape(total_rows, width),
        grad_keys.reshape(total_rows, width),
        grad_values.reshape(total_rows, width),
    )


def block_forward(inputs, live, weights, heads):
    vectors, qkv_weight, out_weight, up_weight, up_bias, down_weight = weights
    gains = vectors.astype(jnp.float32)
    width = inputs.shape[1]
    normed = norm_rows(inputs, gains[0], gains[1]).astype(jnp.bfloat16)
    joined = jnp.dot(normed, qkv_weight, preferred_element_type=jnp.float32)
    queries = (joined[:, :width] + gains[4]).astype(jnp.bfloat16)
    key_rows = joined[:, width : 2 * width].astype(jnp.bfloat16)
    value_rows = (joined[:, 2 * width :] + gains[5]).astype(jnp.bfloat16)
    attended, sums_log = attend_forward(queries, key_rows, value_rows, live, heads)
    attended = attended.astype(jnp.bfloat16)
    middle = inputs + (jnp.dot(attended, out_weight, preferred_element_type=jnp.float32) + gains[6])
    normed_two = norm_rows(middle, gains[2], gains[3]).astype(jnp.bfloat16)
    hidden = jnp.dot(normed_two, up_weight, preferred_element_type=jnp.float32) + up_bias.astype(
        jnp.float32
    )
    active = exact_gelu(hidden).astype(jnp.bfloat16)
    result = middle + (jnp.dot(active, down_weight, preferred_element_type=jnp.float32) + gains[7])
    kept = (
        inputs,
        normed,
        queries,
        key_rows,
        value_rows,
        attended,
        sums_log,
        middle,
        normed_two,
        hidden,
        active,
    )
    return (result, kept)


def block_backward(grad_out, kept, weights, live, heads):
    vectors, qkv_weight, out_weight, up_weight, up_bias, down_weight = weights
    gains = vectors.astype(jnp.float32)
    (
        inputs,
        normed,
        queries,
        key_rows,
        value_rows,
        attended,
        sums_log,
        middle,
        normed_two,
        hidden,
        active,
    ) = kept
    grad_branch = grad_out.astype(jnp.bfloat16)
    grad_down = jnp.einsum("rf,rd->fd", active, grad_branch, preferred_element_type=jnp.float32)
    grad_active = jnp.einsum(
        "rd,fd->rf", grad_branch, down_weight, preferred_element_type=jnp.float32
    )
    unused, gelu_pull = jax.vjp(exact_gelu, hidden)
    grad_hidden = gelu_pull(grad_active)[0].astype(jnp.bfloat16)
    grad_up = jnp.einsum("rd,rf->df", normed_two, grad_hidden, preferred_element_type=jnp.float32)
    grad_normed_two = jnp.einsum(
        "rf,df->rd", grad_hidden, up_weight, preferred_element_type=jnp.float32
    )
    unused, second_pull = jax.vjp(norm_rows, middle, gains[2], gains[3])
    grad_middle, grad_gain_two, grad_shift_two = second_pull(grad_normed_two)
    grad_middle = grad_middle + grad_out
    grad_attn = grad_middle.astype(jnp.bfloat16)
    grad_out_weight = jnp.einsum(
        "rd,re->de", attended, grad_attn, preferred_element_type=jnp.float32
    )
    grad_attended = jnp.einsum(
        "re,de->rd", grad_attn, out_weight, preferred_element_type=jnp.float32
    ).astype(jnp.bfloat16)
    grad_query, grad_keys, grad_values = attend_backward(
        queries, key_rows, value_rows, sums_log, grad_attended, live, heads
    )
    grad_query = grad_query.astype(jnp.bfloat16)
    grad_keys = grad_keys.astype(jnp.bfloat16)
    grad_values = grad_values.astype(jnp.bfloat16)
    grad_joined = jnp.concatenate([grad_query, grad_keys, grad_values], axis=1)
    grad_qkv = jnp.einsum("rd,re->de", normed, grad_joined, preferred_element_type=jnp.float32)
    grad_normed = jnp.einsum(
        "re,de->rd", grad_joined, qkv_weight, preferred_element_type=jnp.float32
    )
    unused, first_pull = jax.vjp(norm_rows, inputs, gains[0], gains[1])
    grad_inputs, grad_gain_one, grad_shift_one = first_pull(grad_normed)
    grad_inputs = grad_inputs + grad_middle
    grad_vectors = jnp.stack(
        [
            grad_gain_one,
            grad_shift_one,
            grad_gain_two,
            grad_shift_two,
            jnp.sum(grad_query.astype(jnp.float32), 0),
            jnp.sum(grad_values.astype(jnp.float32), 0),
            jnp.sum(grad_attn.astype(jnp.float32), 0),
            jnp.sum(grad_branch.astype(jnp.float32), 0),
        ]
    )
    grad_up_bias = jnp.sum(grad_hidden.astype(jnp.float32), 0)
    return (
        grad_inputs,
        (grad_vectors, grad_qkv, grad_out_weight, grad_up, grad_up_bias, grad_down),
    )


def encoder_inputs(rows_in, length):
    keep = jnp.arange(rows_in.shape[0]) < length // 10
    return (jnp.where(keep[:, None], rows_in.astype(jnp.float32), 0.0), keep)


def encoder_back(rows_in, length, grad_encoded, enc_weights):
    inputs, keep = encoder_inputs(rows_in, length)
    unused, kept = block_forward(inputs, keep, enc_weights, HEADS_E)
    grad_inputs, grads = block_backward(
        grad_encoded.astype(jnp.float32), kept, enc_weights, keep, HEADS_E
    )
    return (jnp.where(keep[:, None], grad_inputs, 0.0), grads)


def decode_cube(encoded, length, order, cotan, dec_weights):
    embed_weight, dec_vectors, positions = (dec_weights[0], dec_weights[1], dec_weights[2])
    block_weights = (dec_weights[1],) + tuple(dec_weights[3:])
    gains = dec_vectors.astype(jnp.float32)
    visible_count = encoded.shape[0]
    total_rows = positions.shape[0]
    keep = jnp.arange(visible_count) < length // 10
    places = jnp.where(keep, order[:visible_count], total_rows)
    embedded = jnp.dot(encoded, embed_weight, preferred_element_type=jnp.float32) + gains[8]
    filled = (
        jnp.broadcast_to(gains[9], (total_rows, gains.shape[1]))
        .at[places]
        .set(embedded, mode="drop")
    )
    inputs = filled + positions.astype(jnp.float32)
    live = jnp.arange(total_rows) < length
    result, kept = block_forward(inputs, live, block_weights, HEADS_D)
    result = jnp.where(live[:, None], result, 0.0)
    grad_result = jnp.where(live[:, None], cotan.astype(jnp.float32), 0.0)
    grad_inputs, block_grads = block_backward(grad_result, kept, block_weights, live, HEADS_D)
    picked = jnp.where(
        keep[:, None], jnp.take(grad_inputs, jnp.minimum(places, total_rows - 1), axis=0), 0.0
    )
    grad_embedded = picked.astype(jnp.bfloat16)
    grad_embed = jnp.einsum("rd,re->de", encoded, grad_embedded, preferred_element_type=jnp.float32)
    grad_encoded = jnp.einsum(
        "re,de->rd", grad_embedded, embed_weight, preferred_element_type=jnp.float32
    ).astype(jnp.bfloat16)
    grad_token = jnp.sum(grad_inputs, 0) - jnp.sum(picked, 0)
    extra_rows = jnp.stack([jnp.sum(grad_embedded.astype(jnp.float32), 0), grad_token])
    grad_vectors = jnp.concatenate([block_grads[0], extra_rows], 0)
    grads = (grad_embed, grad_vectors, grad_inputs) + tuple(block_grads[1:])
    return (result.astype(jnp.bfloat16), grad_encoded, grads)


def take_rows(source, places):
    return jnp.take(source, places, axis=0)


def place_rows(rows_in, spots, total_rows):
    return (
        jnp.zeros((total_rows, rows_in.shape[1]), jnp.float32).at[spots].set(rows_in, mode="drop")
    )


def share_each(grads):
    return (
        lax.psum_scatter(grads[0], ("segment", "dp"), scatter_dimension=1, tiled=True),
        lax.psum_scatter(grads[1], ("segment", "dp"), scatter_dimension=0, tiled=True),
        lax.psum_scatter(grads[2], ("segment", "dp"), scatter_dimension=0, tiled=True),
        lax.psum_scatter(grads[3], ("segment", "dp"), scatter_dimension=0, tiled=True),
        lax.psum_scatter(grads[4], ("segment", "dp"), scatter_dimension=0, tiled=True),
        lax.psum_scatter(grads[5], ("segment", "dp"), scatter_dimension=0, tiled=True),
        lax.psum_scatter(grads[6], ("segment", "dp"), scatter_dimension=0, tiled=True),
        lax.psum_scatter(grads[7], ("segment", "dp"), scatter_dimension=1, tiled=True),
        lax.psum_scatter(grads[8], ("segment", "dp"), scatter_dimension=1, tiled=True),
        lax.psum_scatter(grads[9], ("segment", "dp"), scatter_dimension=0, tiled=True),
        lax.psum_scatter(grads[10], ("segment", "dp"), scatter_dimension=0, tiled=True),
        lax.psum_scatter(grads[11], ("segment", "dp"), scatter_dimension=0, tiled=True),
        lax.psum_scatter(grads[12], ("segment", "dp"), scatter_dimension=0, tiled=True),
        lax.psum_scatter(grads[13], ("segment", "dp"), scatter_dimension=0, tiled=True),
    )


def body(
    patches,
    lengths,
    keep_order,
    e_vectors,
    e_qkv,
    e_proj,
    e_fc1,
    e_fc1_bias,
    e_fc2,
    embed,
    d_vectors,
    dec_pos,
    d_qkv,
    d_proj,
    d_fc1,
    d_fc1_bias,
    d_fc2,
    cotangent,
):
    masters = (
        e_vectors,
        e_qkv,
        e_proj,
        e_fc1,
        e_fc1_bias,
        e_fc2,
        embed,
        d_vectors,
        dec_pos,
        d_qkv,
        d_proj,
        d_fc1,
        d_fc1_bias,
        d_fc2,
    )
    first_segment = lax.axis_index("segment") == 0
    later_segment = jnp.logical_not(first_segment)
    gathered = (
        lax.all_gather(e_vectors.astype(jnp.bfloat16), ("segment", "dp"), axis=1, tiled=True),
        lax.all_gather(e_qkv.astype(jnp.bfloat16), ("segment", "dp"), axis=0, tiled=True),
        lax.all_gather(e_proj.astype(jnp.bfloat16), ("segment", "dp"), axis=0, tiled=True),
        lax.all_gather(e_fc1.astype(jnp.bfloat16), ("segment", "dp"), axis=0, tiled=True),
        lax.all_gather(e_fc1_bias.astype(jnp.bfloat16), ("segment", "dp"), axis=0, tiled=True),
        lax.all_gather(e_fc2.astype(jnp.bfloat16), ("segment", "dp"), axis=0, tiled=True),
        lax.all_gather(embed.astype(jnp.bfloat16), ("segment", "dp"), axis=0, tiled=True),
        lax.all_gather(d_vectors.astype(jnp.bfloat16), ("segment", "dp"), axis=1, tiled=True),
        lax.all_gather(dec_pos.astype(jnp.bfloat16), ("segment", "dp"), axis=1, tiled=True),
        lax.all_gather(d_qkv.astype(jnp.bfloat16), ("segment", "dp"), axis=0, tiled=True),
        lax.all_gather(d_proj.astype(jnp.bfloat16), ("segment", "dp"), axis=0, tiled=True),
        lax.all_gather(d_fc1.astype(jnp.bfloat16), ("segment", "dp"), axis=0, tiled=True),
        lax.all_gather(d_fc1_bias.astype(jnp.bfloat16), ("segment", "dp"), axis=0, tiled=True),
        lax.all_gather(d_fc2.astype(jnp.bfloat16), ("segment", "dp"), axis=0, tiled=True),
    )
    enc_weights = tuple(gathered[:6])
    dec_weights = tuple(gathered[6:])
    pair_count = lax.axis_size("dp")
    rank_id = lax.axis_index("dp")
    own_count = patches.shape[0]
    total_slots = keep_order.shape[1]
    low_base = rank_id * own_count
    high_base = (pair_count + rank_id) * own_count
    own_base = jnp.where(first_segment, low_base, high_base)
    own_orders = lax.dynamic_slice_in_dim(keep_order, own_base, own_count, 0)[:, :VIS]
    own_lengths = lax.dynamic_slice_in_dim(lengths, own_base, own_count, 0)
    picked_rows = jax.vmap(take_rows)(patches, own_orders)
    arrived = shifted(picked_rows, "segment", -1)
    pair_rows = jnp.concatenate([picked_rows, arrived], 0)
    pair_lengths = jnp.concatenate(
        [
            lax.dynamic_slice_in_dim(lengths, low_base, own_count, 0),
            lax.dynamic_slice_in_dim(lengths, high_base, own_count, 0),
        ],
        0,
    )
    pair_orders = jnp.concatenate(
        [
            lax.dynamic_slice_in_dim(keep_order, low_base, own_count, 0),
            lax.dynamic_slice_in_dim(keep_order, high_base, own_count, 0),
        ],
        0,
    )

    def encoder_all(rows_all):

        def encode_one(pieces):
            inputs, keep = encoder_inputs(pieces[0], pieces[1])
            result, unused = block_forward(inputs, keep, enc_weights, HEADS_E)
            return result.astype(jnp.bfloat16)

        return lax.map(encode_one, (rows_all, pair_lengths))

    encoded = lax.cond(first_segment, encoder_all, jnp.zeros_like, pair_rows)
    encoded_in, cotan_low = shifted((encoded, cotangent), "segment", 1)
    pair_cotan = jnp.concatenate([cotan_low, cotangent], 0)

    def decoder_run(pieces):
        return decode_cube(pieces[0], pieces[1], pieces[2], pieces[3], dec_weights)

    def decoder_skip(pieces):
        return (
            jnp.zeros((total_slots, dec_weights[1].shape[1]), jnp.bfloat16),
            jnp.zeros_like(pieces[0]),
            tuple((jnp.zeros(weight.shape, jnp.float32) for weight in dec_weights)),
        )

    def encoder_run(pieces):
        return encoder_back(pieces[0], pieces[1], pieces[2], enc_weights)

    def encoder_skip(pieces):
        return (
            jnp.zeros(pieces[0].shape, jnp.float32),
            tuple((jnp.zeros(weight.shape, jnp.float32) for weight in enc_weights)),
        )

    shards = tuple((jnp.zeros(master.shape, jnp.float32) for master in masters))
    results = []
    row_grads = []
    for cube_pos in range(2 * own_count):
        decoded_one, grad_encoded, dec_grads = lax.cond(
            later_segment,
            decoder_run,
            decoder_skip,
            (
                encoded_in[cube_pos],
                pair_lengths[cube_pos],
                pair_orders[cube_pos],
                pair_cotan[cube_pos],
            ),
        )
        returned = shifted(grad_encoded, "segment", -1)
        grad_rows, enc_grads = lax.cond(
            first_segment,
            encoder_run,
            encoder_skip,
            (pair_rows[cube_pos], pair_lengths[cube_pos], returned),
        )
        step_grads = tuple(enc_grads) + tuple(dec_grads)
        pieces_now = share_each(step_grads)
        shards = tuple((before + added for before, added in zip(shards, pieces_now)))
        results.append(decoded_one)
        row_grads.append(grad_rows)
    low_results = shifted(jnp.stack(results[:own_count]), "segment", -1)
    decoded = jnp.where(first_segment, low_results, jnp.stack(results[own_count:]))
    high_rows = shifted(jnp.stack(row_grads[own_count:]).astype(jnp.bfloat16), "segment", 1).astype(
        jnp.float32
    )
    my_rows = jnp.where(first_segment, jnp.stack(row_grads[:own_count]), high_rows)
    keep_slots = jnp.arange(VIS)[None, :] < (own_lengths // 10)[:, None]
    spots = jnp.where(keep_slots, own_orders, total_slots)
    patch_grads = jax.vmap(lambda rows_in, spot_list: place_rows(rows_in, spot_list, total_slots))(
        my_rows, spots
    )
    return (decoded, patch_grads) + tuple(shards)


def solution(mesh):
    return jax.shard_map(
        body,
        mesh=mesh,
        in_specs=(
            P(("segment", "dp"), None, None),
            P(),
            P(),
            P(None, ("segment", "dp")),
            P(("segment", "dp"), None),
            P(("segment", "dp"), None),
            P(("segment", "dp"), None),
            P(("segment", "dp")),
            P(("segment", "dp"), None),
            P(("segment", "dp"), None),
            P(None, ("segment", "dp")),
            P(None, ("segment", "dp")),
            P(("segment", "dp"), None),
            P(("segment", "dp"), None),
            P(("segment", "dp"), None),
            P(("segment", "dp")),
            P(("segment", "dp"), None),
            P(("segment", "dp"), None, None),
        ),
        out_specs=(
            P(("segment", "dp"), None, None),
            P(("segment", "dp"), None, None),
            P(None, ("segment", "dp")),
            P(("segment", "dp"), None),
            P(("segment", "dp"), None),
            P(("segment", "dp"), None),
            P(("segment", "dp")),
            P(("segment", "dp"), None),
            P(("segment", "dp"), None),
            P(None, ("segment", "dp")),
            P(None, ("segment", "dp")),
            P(("segment", "dp"), None),
            P(("segment", "dp"), None),
            P(("segment", "dp"), None),
            P(("segment", "dp")),
            P(("segment", "dp"), None),
        ),
        check_vma=False,
    )
```

profile of v0, /device:TPU:0, one launch (start us, length us, event | category | flops | bytes accessed | tf_op | source)
XLA Modules:
  0.0 2802.9 jit_solution(18318777653439573897)
XLA Ops:
  29.7 44.3 %all_gather.52 = bf16[512,512]{1,0:T(8,128)(2,1)} all-gather(bf16[16,512]{1,0:T(8,128)(2,1)S(1)} %convert_element_type.651), channel_id=1, replica_groups=mesh['segment'=2,'dp'=16] {'segment','dp'}, dimensions={0}, use_global_device_ids=true | all-gather | bytes 540672 | tf_op jit(solution)/shard_map/all_gather | solution.py:340
  74.2 36.9 %all-gather = bf16[32,24,8]{1,2,0:T(8,128)(2,1)S(1)} all-gather(bf16[1,24,8]{1,2,0:T(8,128)(2,1)S(1)} %convert_bitcast_fusion.1), channel_id=1, replica_groups=mesh['segment'=2,'dp'=16] {'segment','dp'}, dimensions={0}, use_global_device_ids=true | all-gather | bytes 12672 | tf_op jit(solution)/shard_map/all_gather | solution.py:330
  113.0 40.5 %all-reduce.6 = (bf16[3072]{0:T(1024)(128)(2,1)}, bf16[2048]{0:T(1024)(128)(2,1)S(1)}) all-reduce(bf16[3072]{0:T(1024)(128)(2,1)S(1)} %dynamic-update-slice, bf16[2048]{0:T(1024)(128)(2,1)S(1)} %dynamic-update-slice.1), channel_id=1, replica_groups=mesh['segment'=2,'dp'=16] {'segment','dp'}, use_global_device_ids=true, to_apply=%add | all-reduce | flops 5120 | bytes 20480
  153.4 41.4 %all_gather.42 = bf16[10,512]{0,1:T(8,128)(2,1)S(1)} all-gather(bf16[10,16]{0,1:T(8,128)(2,1)S(1)} %copy.188), channel_id=1, replica_groups=mesh['segment'=2,'dp'=16] {'segment','dp'}, dimensions={1}, use_global_device_ids=true | all-gather | bytes 10560 | tf_op jit(solution)/shard_map/all_gather | solution.py:337
  198.4 65.8 %all-gather.16.cloned.1.call-done = bf16[3072,768]{1,0:T(8,128)(2,1)} async-done(((bf16[96,768]{1,0:T(8,128)(2,1)}), bf16[3072,768]{1,0:T(8,128)(2,1)}) %all-gather.16.cloned.1.call-update) | async-done | bytes 4718608 | tf_op jit(solution)/shard_map/all_gather | solution.py:335
  264.2 37.4 %conditional.5 = (bf16[2,104,768]{2,1,0:T(8,128)(2,1)}) conditional(s32[]{:T(128)} %convert_element_type.641, () %tuple.94, (s32[2]{0:T(128)S(1)}, bf16[2,104,768]{2,1,0:T(8,128)(2,1)S(1)}, bf16[8,768]{1,0:T(8,128)(2,1)}, bf16[768,2304]{1,0:T(8,128)(2,1)}, bf16[768,768]{1,0:T(8,128)(2,1)}, /*index=5*/bf16[768,3072]{1,0:T(8,128)(2,1)}, ...), branch_computations={%region_0.1_spmd, %region_1.10_spmd} | conditional | flops 1547183104 | bytes 26468316 | solution.py:383
  264.2 37.4 %while.111 = (s32[]{:T(128)}, bf16[2,104,768]{2,1,0:T(8,128)(2,1)}, s32[2]{0:T(128)S(1)}, bf16[2,104,768]{2,1,0:T(8,128)(2,1)S(1)}, bf16[8,768]{1,0:T(8,128)(2,1...) while((s32[]{:T(128)}, bf16[2,104,768]{2,1,0:T(8,128)(2,1)}, ...), condition=%wide.region_9.9_spmd, body=%wide.region_2.8_spmd.sunk | while | flops 1547183104 | bytes 26468180 | solution.py:381
  274.4 8.5 fusion.597
  293.1 8.5 fusion.597
  302.9 40.9 %all_gather.49 = bf16[768,512]{1,0:T(8,128)(2,1)S(1)} all-gather(bf16[24,512]{1,0:T(8,128)(2,1)S(1)} %convert_element_type.648), channel_id=1, replica_groups=mesh['segment'=2,'dp'=16] {'segment','dp'}, dimensions={0}, use_global_device_ids=true | all-gather | bytes 811008 | tf_op jit(solution)/shard_map/all_gather | solution.py:336
  343.8 35.1 %all-gather.20.cloned.1.call-done = bf16[512,1536]{1,0:T(8,128)(2,1)} async-done(((bf16[16,1536]{1,0:T(8,128)(2,1)}), bf16[512,1536]{1,0:T(8,128)(2,1)}) %all-gather.20.cloned.1.call-update) | async-done | bytes 1572880 | tf_op jit(solution)/shard_map/all_gather | solution.py:339
  378.9 58.8 %all-gather.22.cloned.1.call-done = bf16[512,2048]{1,0:T(8,128)(2,1)} async-done(((bf16[16,2048]{1,0:T(8,128)(2,1)}), bf16[512,2048]{1,0:T(8,128)(2,1)}) %all-gather.22.cloned.1.call-update) | async-done | bytes 2097168 | tf_op jit(solution)/shard_map/all_gather | solution.py:341
  437.7 58.8 %all-gather.24.cloned.1.call-done = bf16[2048,512]{1,0:T(8,128)(2,1)} async-done(((bf16[64,512]{1,0:T(8,128)(2,1)}), bf16[2048,512]{1,0:T(8,128)(2,1)}) %all-gather.24.cloned.1.call-update) | async-done | bytes 2097168 | tf_op jit(solution)/shard_map/all_gather | solution.py:343
  497.2 16.7 conditional.6
  513.9 20.5 conditional.7
  545.1 861.5 %collective-permute-done.5 = bf16[104,768]{1,0:T(8,128)(2,1)S(1)} collective-permute-done((bf16[104,768]{1,0:T(8,128)(2,1)}, bf16[104,768]{1,0:T(8,128)(2,1)S(1)}, u32[]{:S(2)}, u32[]{:S(2)}) %collective-permute-start.5) | collective-permute-done | bytes 159776 | tf_op jit(solution)/shard_map/ppermute | solution.py:18
  1406.6 40.8 %conditional.9 = (bf16[104,768]{1,0:T(8,128)(2,1)}, f32[8,768]{1,0:T(8,128)S(1)}, f32[768,2304]{1,0:T(8,128)S(1)}, f32[768,768]{1,0:T(8,128)S(1)}, f32[768,3072]...) conditional(s32[]{:T(128)} %convert_element_type.641, () %tuple.101, (s32[]{:T(128)}, ...), branch_computations={%region_92.94_spmd, %region_93.0_spmd} | conditional | flops 4083506688 | bytes 133951872 | solution.py:422
  1456.8 52.3 %conditional.8 = (f32[8,768]{1,0:T(8,128)S(1)}, f32[768,2304]{1,0:T(8,128)}, f32[768,768]{1,0:T(8,128)S(1)}, f32[768,3072]{1,0:T(8,128)}, f32[3072]{0:T(1024)S(1...) conditional(s32[]{:T(128)} %convert_element_type.641, () %tuple.99, (s32[]{:T(128)}, ...), branch_computations={%region_70.72_spmd, %region_71.93_spmd} | conditional | flops 4084065792 | bytes 129787712 | solution.py:422
  1496.5 7.3 fusion.262
  1535.5 8.9 add.999
  1544.5 13.1 add.1001
  1557.6 11.4 add.1003
  1581.9 51.7 %all-reduce.5 = (f32[8,768]{1,0:T(8,128)S(1)}, f32[3072]{0:T(1024)S(1)}, f32[2048]{0:T(1024)S(1)}) all-reduce(f32[8,768]{1,0:T(8,128)S(1)} %add.998, f32[3072]{0:T(1024)S(1)} %add.1002, f32[2048]{0:T(1024)S(1)} %add.1010), channel_id=16, replica_groups=mesh['segment'=2,'dp'=16] {'segment','dp'}, use_global_device_ids=true, to_apply=%region_115.117.clone | all-reduce | flops 11264 | bytes 90112
  1639.4 125.2 %reduce-scatter.29.cloned.1.call-done = f32[16,512]{1,0:T(8,128)} async-done(((f32[512,512]{1,0:T(8,128)}), f32[16,512]{1,0:T(8,128)}) %reduce-scatter.29.cloned.1.call-update) | async-done | bytes 32784 | tf_op jit(solution)/shard_map/reduce_scatter | solution.py:284
  1764.6 101.1 %reduce-scatter.17.cloned.1.call-done = f32[24,768]{1,0:T(8,128)} async-done(((f32[768,768]{1,0:T(8,128)}), f32[24,768]{1,0:T(8,128)}) %reduce-scatter.17.cloned.1.call-update) | async-done | bytes 73744 | tf_op jit(solution)/shard_map/reduce_scatter | solution.py:276
  1865.6 138.9 %reduce-scatter.25.cloned.1.call-done = f32[1024,16]{0,1:T(8,128)} async-done(((f32[1024,512]{0,1:T(8,128)}), f32[1024,16]{0,1:T(8,128)}) %reduce-scatter.25.cloned.1.call-update) | async-done | bytes 65552 | tf_op jit(solution)/shard_map/reduce_scatter | solution.py:282
  2004.5 103.3 %reduce-scatter.27.cloned.1.call-done = f32[16,1536]{1,0:T(8,128)} async-done(((f32[512,1536]{1,0:T(8,128)}), f32[16,1536]{1,0:T(8,128)}) %reduce-scatter.27.cloned.1.call-update) | async-done | bytes 98320 | tf_op jit(solution)/shard_map/reduce_scatter | solution.py:283
  2107.8 142.7 %reduce-scatter.31.cloned.1.call-done = f32[16,2048]{1,0:T(8,128)} async-done(((f32[512,2048]{1,0:T(8,128)}), f32[16,2048]{1,0:T(8,128)}) %reduce-scatter.31.cloned.1.call-update) | async-done | bytes 131088 | tf_op jit(solution)/shard_map/reduce_scatter | solution.py:285
  2250.5 140.4 %reduce-scatter.33.cloned.1.call-done = f32[64,512]{1,0:T(8,128)} async-done(((f32[2048,512]{1,0:T(8,128)}), f32[64,512]{1,0:T(8,128)}) %reduce-scatter.33.cloned.1.call-update) | async-done | bytes 131088 | tf_op jit(solution)/shard_map/reduce_scatter | solution.py:287
  2391.0 121.7 %reduce-scatter.15.cloned.1.call-done = f32[24,2304]{1,0:T(8,128)} async-done(((f32[768,2304]{1,0:T(8,128)}), f32[24,2304]{1,0:T(8,128)}) %reduce-scatter.15.cloned.1.call-update) | async-done | bytes 221200 | tf_op jit(solution)/shard_map/reduce_scatter | solution.py:275
  2512.7 142.2 %reduce-scatter.19.cloned.1.call-done = f32[24,3072]{1,0:T(8,128)} async-done(((f32[768,3072]{1,0:T(8,128)}), f32[24,3072]{1,0:T(8,128)}) %reduce-scatter.19.cloned.1.call-update) | async-done | bytes 294928 | tf_op jit(solution)/shard_map/reduce_scatter | solution.py:277
  2654.9 141.3 %reduce-scatter.21.cloned.1.call-done = f32[96,768]{1,0:T(8,128)} async-done(((f32[3072,768]{1,0:T(8,128)}), f32[96,768]{1,0:T(8,128)}) %reduce-scatter.21.cloned.1.call-update) | async-done | bytes 294928 | tf_op jit(solution)/shard_map/reduce_scatter | solution.py:279
  (436 shorter events, 218.1 us)
Async XLA Ops:
  7.2 189.0 %all-gather.12.cloned.1.call-start = ((), (), s32[]{:S(2)}) async-start(), calls=%async_computation.12 | async-start | bytes 1216512 | tf_op jit(solution)/shard_map/all_gather | solution.py:332
  8.9 187.3 %all-gather.10.cloned.1.call-start = ((), (), s32[]{:S(2)}) async-start(), calls=%async_computation.11 | async-start | bytes 3649536 | tf_op jit(solution)/shard_map/all_gather | solution.py:331
  10.7 187.7 %all-gather.14.cloned.1.call-start = ((), (), s32[]{:S(2)}) async-start(), calls=%async_computation.13 | async-start | bytes 4866048 | tf_op jit(solution)/shard_map/all_gather | solution.py:333
  12.4 251.8 %all-gather.16.cloned.1.call-start = ((), (), s32[]{:S(2)}) async-start(), calls=%async_computation.14 | async-start | bytes 4866048 | tf_op jit(solution)/shard_map/all_gather | solution.py:335
  14.1 329.7 %all-gather.18.cloned.1.call-start = ((), (), s32[]{:S(2)}) async-start(), calls=%async_computation.15 | async-start | bytes 1081344 | tf_op jit(solution)/shard_map/all_gather | solution.py:338
  15.6 363.3 %all-gather.20.cloned.1.call-start = ((), (), s32[]{:S(2)}) async-start(), calls=%async_computation.16 | async-start | bytes 1622016 | tf_op jit(solution)/shard_map/all_gather | solution.py:339
  17.2 420.5 %all-gather.22.cloned.1.call-start = ((), (), s32[]{:S(2)}) async-start(), calls=%async_computation.17 | async-start | bytes 2162688 | tf_op jit(solution)/shard_map/all_gather | solution.py:341
  18.0 478.5 %all-gather.24.cloned.1.call-start = ((), (), s32[]{:S(2)}) async-start(), calls=%async_computation.18 | async-start | bytes 2162688 | tf_op jit(solution)/shard_map/all_gather | solution.py:343
  18.8 1561.8 %reduce-scatter.35.cloned.1.call-start = ((), (), s32[]{:S(2)}) async-start(), calls=%async_computation.29 | async-start | bytes 270336
  21.1 175.1 %copy-start.40 = (bf16[104,768]{1,0:T(8,128)(2,1)}, bf16[104,768]{1,0:T(8,128)(2,1)S(1)}, u32[]{:S(2)}) copy-start(bf16[104,768]{1,0:T(8,128)(2,1)S(1)} %gather_fusion.2) | copy-start | bytes 479236
  21.2 175.0 %collective-permute-start = (bf16[1,104,768]{2,1,0:T(8,128)(2,1)S(1)}, bf16[1,104,768]{2,1,0:T(8,128)(2,1)S(1)}, u32[]{:S(2)}, u32[]{:S(2)}) collective-permute-start(bf16[1,104,768]{2,1,0:T(8,128)(2,1)S(1)} %broadcast_select_fusion.1), channel_id=1, source_target_pairs={{16,0},{17,1},{18,2},{19,3},{20,4},{21,5},{22,6},{23,7},{24,8},{25... | collective-permute-start | bytes 479240 | tf_op jit(solution)/shard_map/ppermute | solution.py:18
  23.9 320.0 %collective-permute-start.2 = (bf16[1,1024,512]{1,2,0:T(8,128)(2,1)}, bf16[1,1024,512]{1,2,0:T(8,128)(2,1)}, u32[]{:S(2)}, u32[]{:S(2)}) collective-permute-start(bf16[1,1024,512]{1,2,0:T(8,128)(2,1)} %copy.190), channel_id=1, source_target_pairs={{0,16},{1,17},{2,18},{3,19},{4,20},{5,21},{6,22},{7,23},{8,24},{9,... | collective-permute-start | bytes 3145736 | tf_op jit(solution)/shard_map/ppermute | solution.py:18
  153.4 343.0 %copy-start.131 = (bf16[2048]{0:T(1024)(128)(2,1)}, bf16[2048]{0:T(1024)(128)(2,1)S(1)}, u32[]{:S(2)}) copy-start(bf16[2048]{0:T(1024)(128)(2,1)S(1)} %get-tuple-element.1120) | copy-start | bytes 12292
  301.6 194.9 %collective-permute-start.1 = (bf16[2,104,768]{2,1,0:T(8,128)(2,1)}, bf16[2,104,768]{2,1,0:T(8,128)(2,1)S(1)}, u32[]{:S(2)}, u32[]{:S(2)}) collective-permute-start(bf16[2,104,768]{2,1,0:T(8,128)(2,1)} %get-tuple-element.1861), channel_id=1, source_target_pairs={{0,16},{1,17},{2,18},{3,19},{4,20},{5,21},{6,22},{7,23},{8,24},{9,... | collective-permute-start | bytes 958472 | tf_op jit(solution)/shard_map/ppermute | solution.py:18
  343.8 152.6 %copy-start.30 = (bf16[768,512]{1,0:T(8,128)(2,1)}, bf16[768,512]{1,0:T(8,128)(2,1)S(1)}, u32[]{:S(2)}) copy-start(bf16[768,512]{1,0:T(8,128)(2,1)S(1)} %all_gather.49) | copy-start | bytes 2359300
  536.1 1103.3 %reduce-scatter.23.cloned.1.call-start = ((), (), s32[]{:S(2)}) async-start(), calls=%async_computation.23 | async-start | bytes 1622016 | tf_op jit(solution)/shard_map/reduce_scatter | solution.py:280
  539.6 1225.0 %reduce-scatter.29.cloned.1.call-start = ((), (), s32[]{:S(2)}) async-start(), calls=%async_computation.26 | async-start | bytes 1081344 | tf_op jit(solution)/shard_map/reduce_scatter | solution.py:284
  539.6 867.0 %copy-start.8 = (bf16[768,768]{1,0:T(8,128)(2,1)S(1)}, bf16[768,768]{1,0:T(8,128)(2,1)}, u32[]{:S(2)}) copy-start(bf16[768,768]{1,0:T(8,128)(2,1)} %all-gather.12.cloned.1.call-done) | copy-start | bytes 3538948
  539.6 867.0 %copy-start.48 = (bf16[1,104,768]{2,1,0:T(8,128)(2,1)S(1)}, bf16[1,104,768]{2,1,0:T(8,128)(2,1)}, u32[]{:S(2)}) copy-start(bf16[1,104,768]{2,1,0:T(8,128)(2,1)} %copy-done.47) | copy-start | bytes 479236
  542.5 1323.2 %reduce-scatter.17.cloned.1.call-start = ((), (), s32[]{:S(2)}) async-start(), calls=%async_computation.20 | async-start | bytes 2433024 | tf_op jit(solution)/shard_map/reduce_scatter | solution.py:276
  542.5 864.1 %collective-permute-start.5 = (bf16[104,768]{1,0:T(8,128)(2,1)}, bf16[104,768]{1,0:T(8,128)(2,1)S(1)}, u32[]{:S(2)}, u32[]{:S(2)}) collective-permute-start(bf16[104,768]{1,0:T(8,128)(2,1)} %get-tuple-element.739), channel_id=1, source_target_pairs={{16,0},{17,1},{18,2},{19,3},{20,4},{21,5},{22,6},{23,7},{24,8},{25... | collective-permute-start | bytes 479240 | tf_op jit(solution)/shard_map/ppermute | solution.py:18
  543.8 903.7 %collective-permute-start.4 = (bf16[104,768]{1,0:T(8,128)(2,1)}, bf16[104,768]{1,0:T(8,128)(2,1)}, u32[]{:S(2)}, u32[]{:S(2)}) collective-permute-start(bf16[104,768]{1,0:T(8,128)(2,1)} %get-tuple-element.737), channel_id=1, source_target_pairs={{16,0},{17,1},{18,2},{19,3},{20,4},{21,5},{22,6},{23,7},{24,8},{25... | collective-permute-start | bytes 479240 | tf_op jit(solution)/shard_map/ppermute | solution.py:18
  1512.7 491.8 %reduce-scatter.25.cloned.1.call-start = ((), (), s32[]{:S(2)}) async-start(), calls=%async_computation.24 | async-start | bytes 2162688 | tf_op jit(solution)/shard_map/reduce_scatter | solution.py:282
  1516.9 590.9 %reduce-scatter.27.cloned.1.call-start = ((), (), s32[]{:S(2)}) async-start(), calls=%async_computation.25 | async-start | bytes 3244032 | tf_op jit(solution)/shard_map/reduce_scatter | solution.py:283
  1522.2 728.4 %reduce-scatter.31.cloned.1.call-start = ((), (), s32[]{:S(2)}) async-start(), calls=%async_computation.27 | async-start | bytes 4325376 | tf_op jit(solution)/shard_map/reduce_scatter | solution.py:285
  1528.9 862.1 %reduce-scatter.33.cloned.1.call-start = ((), (), s32[]{:S(2)}) async-start(), calls=%async_computation.28 | async-start | bytes 4325376 | tf_op jit(solution)/shard_map/reduce_scatter | solution.py:287
  1535.4 977.3 %reduce-scatter.15.cloned.1.call-start = ((), (), s32[]{:S(2)}) async-start(), calls=%async_computation.19 | async-start | bytes 7299072 | tf_op jit(solution)/shard_map/reduce_scatter | solution.py:275
  1544.4 1110.5 %reduce-scatter.19.cloned.1.call-start = ((), (), s32[]{:S(2)}) async-start(), calls=%async_computation.21 | async-start | bytes 9732096 | tf_op jit(solution)/shard_map/reduce_scatter | solution.py:277
  1557.6 1238.5 %reduce-scatter.21.cloned.1.call-start = ((), (), s32[]{:S(2)}) async-start(), calls=%async_computation.22 | async-start | bytes 9732096 | tf_op jit(solution)/shard_map/reduce_scatter | solution.py:279
  1571.4 66.8 %collective-permute-start.3 = (bf16[1,1024,512]{2,1,0:T(8,128)(2,1)}, bf16[1,1024,512]{2,1,0:T(8,128)(2,1)S(1)}, u32[]{:S(2)}, u32[]{:S(2)}) collective-permute-start(bf16[1,1024,512]{2,1,0:T(8,128)(2,1)} %bitcast.108), channel_id=1, source_target_pairs={{16,0},{17,1},{18,2},{19,3},{20,4},{21,5},{22,6},{23,7},{24,8},{25... | collective-permute-start | bytes 3145736 | tf_op jit(solution)/shard_map/ppermute | solution.py:18
  1575.1 60.3 %collective-permute-start.6 = (bf16[1,104,768]{2,1,0:T(8,128)(2,1)}, bf16[1,104,768]{2,1,0:T(8,128)(2,1)S(1)}, u32[]{:S(2)}, u32[]{:S(2)}) collective-permute-start(bf16[1,104,768]{2,1,0:T(8,128)(2,1)} %bitcast.292), channel_id=1, source_target_pairs={{0,16},{1,17},{2,18},{3,19},{4,20},{5,21},{6,22},{7,23},{8,24},{9,... | collective-permute-start | bytes 479240 | tf_op jit(solution)/shard_map/ppermute | solution.py:18
  1635.5 1160.7 %copy-start.1 = (bf16[1,1024,768]{2,1,0:T(8,128)(2,1)S(1)}, bf16[1,1024,768]{2,1,0:T(8,128)(2,1)}, u32[]{:S(2)}) copy-start(bf16[1,1024,768]{2,1,0:T(8,128)(2,1)} %param.40) | copy-start | bytes 4718596
  (72 other events, 912.3 us)
Sparse Core Ops, SparseCore 0:
  11.5 57.6 all-gather.11
  72.7 59.6 all-gather.9
  135.9 62.4 all-gather.13
  201.7 62.3 all-gather.15
  267.5 53.0 all-gather.17
  323.9 54.9 all-gather.19
  382.4 55.2 all-gather.21
  441.1 55.2 all-gather.23
  536.2 988.6 reduce-scatter.34
  1531.5 96.2 reduce-scatter.22
  1630.7 133.8 reduce-scatter.28
  1770.3 95.3 reduce-scatter.16
  1868.6 135.8 reduce-scatter.24
  2010.4 97.4 reduce-scatter.26
  2110.5 139.9 reduce-scatter.30
  2253.2 137.6 reduce-scatter.32
  2397.1 115.5 reduce-scatter.14
  2520.0 134.7 reduce-scatter.18
  2661.3 134.7 reduce-scatter.20
where the time goes:
time: 2810 us; the launch traced here: 2800 us
  waiting for transfers between devices  2240 us (80%)
  blocking collectives  256 us (9%)
  other arithmetic  99.2 us (4%)
  matrix products  92.6 us (3%)
  local copies, waits for them, and re-layouts  63.9 us (2%)
    ppermute x7, waiting for transfers between devices, shifted(): lax.ppermute(value, axis, [(source, source + steps) for source in range(f...  861 us
    reduce_scatter x1, waiting for transfers between devices, share_each(): lax.psum_scatter(grads[11], ('segment', 'dp'), scatter_dimension=0, tiled...  143 us
    reduce_scatter x1, waiting for transfers between devices, share_each(): lax.psum_scatter(grads[3], ('segment', 'dp'), scatter_dimension=0, tiled=...  142 us
    reduce_scatter x1, waiting for transfers between devices, share_each(): lax.psum_scatter(grads[5], ('segment', 'dp'), scatter_dimension=0, tiled=...  141 us
    reduce_scatter x1, waiting for transfers between devices, share_each(): lax.psum_scatter(grads[13], ('segment', 'dp'), scatter_dimension=0, tiled...  140 us
    reduce_scatter x1, waiting for transfers between devices, share_each(): lax.psum_scatter(grads[8], ('segment', 'dp'), scatter_dimension=1, tiled=...  139 us
    reduce_scatter x1, waiting for transfers between devices, share_each(): lax.psum_scatter(grads[10], ('segment', 'dp'), scatter_dimension=0, tiled...  125 us
    reduce_scatter x1, waiting for transfers between devices, share_each(): lax.psum_scatter(grads[1], ('segment', 'dp'), scatter_dimension=0, tiled=...  122 us
  transfers between devices with their start and end apart: 26, of which 15 were waited for; matrix products, arithmetic and copies ran while one was open for 7% of the time, Pallas kernels for 0%

commit v1 on v0

v1 whole, which is shorter than its diff:
```python
import functools
import math

import jax
import jax.numpy as jnp
from jax import lax
from jax.experimental import pallas as pl
from jax.experimental.pallas import tpu as pltpu
from jax.sharding import PartitionSpec as P

HEADS_E = 12
HEADS_D = 16
VIS = 104
SHORT = 576
HD = 32
GROUP = 128
F32 = jnp.float32
BF16 = jnp.bfloat16
AXES = ("segment", "dp")
MESH = pl.DeviceIdType.MESH
NORM_EPS = 1e-06
FAR_BELOW = -1e30


def place():
    s = lax.axis_index("segment")
    dp = lax.axis_index("dp")
    return s, dp // 4, (dp // 2) % 2, dp % 2


def device(s, z, y, c):
    return (s, (z * 2 + y) * 2 + c)


def halves(columns):
    return (columns // 2, columns // 2) if columns % 256 == 0 else (columns, 0)


def greet(peers):
    barrier = pltpu.get_barrier_semaphore()
    for peer in peers:
        pl.semaphore_signal(barrier, inc=1, device_id=peer, device_id_type=MESH)
    pl.semaphore_wait(barrier, len(peers))


def send(src, dst, send_sem, recv_sem, target):
    copy = pltpu.make_async_remote_copy(
        src_ref=src,
        dst_ref=dst,
        send_sem=send_sem,
        recv_sem=recv_sem,
        device_id=target,
        device_id_type=MESH,
    )
    copy.start()
    return copy


def gather_kernel(n, Z, *refs):
    ins, outs = refs[:n], refs[n : 2 * n]
    loc, zs, zr, ms, mr, cs, cr = refs[2 * n :]
    s, z, y, c = place()
    X, Y, C = device(1 - s, z, y, c), device(s, z, 1 - y, c), device(s, z, y, 1 - c)
    z_peers = [device(s, lax.rem(z + d, Z), y, c) for d in range(1, Z)]
    greet(z_peers + [X, Y, C])
    state = {}
    sends = []

    def both(ref, i, sems, k, target):
        copy = send(ref, ref, sems[0].at[i, k], sems[1].at[i, k], target)
        sends.append(copy)
        return copy

    def stage0(i):
        own = pltpu.make_async_copy(ins[i], outs[i].at[s, z, y, c], loc.at[i])
        own.start()
        copies = [
            send(ins[i], outs[i].at[s, z, y, c], zs.at[i, d], zr.at[i, d], z_peers[d])
            for d in range(Z - 1)
        ]
        sends.extend(copies)
        state[i, 0] = (own, copies)

    def stage1(i):
        own, copies = state[i, 0]
        own.wait()
        for copy in copies:
            copy.wait_recv()
        o = outs[i]
        ka, kb = halves(o.shape[-1])
        A, B = pl.ds(0, ka), pl.ds(ka, kb)
        state[i, 1] = [both(o.at[s, :, y, c, :, A], i, (ms, mr), 0, X)]
        if kb:
            state[i, 1].append(both(o.at[s, :, y, c, :, B], i, (ms, mr), 1, Y))
        state[i, 9] = [both(o.at[s, :, y, c], i, (cs, cr), 0, C)]

    def stage2(i):
        for copy in state[i, 1]:
            copy.wait_recv()
        o = outs[i]
        ka, kb = halves(o.shape[-1])
        A, B = pl.ds(0, ka), pl.ds(ka, kb)
        state[i, 2] = [both(o.at[:, :, y, c, :, A], i, (ms, mr), 2, Y)]
        state[i, 9].append(both(o.at[1 - s, :, y, c, :, A], i, (cs, cr), 1, C))
        if kb:
            state[i, 2].append(both(o.at[s, :, :, c, :, B], i, (ms, mr), 3, X))
            state[i, 9].append(both(o.at[s, :, 1 - y, c, :, B], i, (cs, cr), 2, C))

    def stage3(i):
        for copy in state[i, 2]:
            copy.wait_recv()
        o = outs[i]
        ka, kb = halves(o.shape[-1])
        A, B = pl.ds(0, ka), pl.ds(ka, kb)
        state[i, 9].append(both(o.at[:, :, 1 - y, c, :, A], i, (cs, cr), 3, C))
        if kb:
            state[i, 9].append(both(o.at[1 - s, :, :, c, :, B], i, (cs, cr), 4, C))

    stages = (stage0, stage1, stage2, stage3)
    for t in range(n + 3):
        for k in range(4):
            if 0 <= t - k < n:
                stages[k](t - k)
    for i in range(n):
        for copy in state[i, 9]:
            copy.wait_recv()
    for copy in sends:
        copy.wait_send()


def gather_all(arrays, Z):
    n = len(arrays)
    D = pltpu.SemaphoreType.DMA
    return pl.pallas_call(
        functools.partial(gather_kernel, n, Z),
        out_shape=[jax.ShapeDtypeStruct((2, Z, 2, 2) + a.shape, a.dtype) for a in arrays],
        in_specs=[pl.BlockSpec(memory_space=pl.ANY)] * n,
        out_specs=[pl.BlockSpec(memory_space=pl.ANY)] * n,
        scratch_shapes=[
            D((n,)),
            D((n, Z - 1)),
            D((n, Z - 1)),
            D((n, 4)),
            D((n, 4)),
            D((n, 5)),
            D((n, 5)),
        ],
        compiler_params=pltpu.CompilerParams(collective_id=0, has_side_effects=True),
    )(*arrays)


def scatter_kernel(n, Z, *refs):
    ins, outs = refs[:n], refs[n : 2 * n]
    L0, R0, R1A, R1B, R2A, R2B, R3 = [refs[(2 + i) * n : (3 + i) * n] for i in range(7)]
    loc, cs, cr, ms, mr, zs, zr = refs[9 * n :]
    s, z, y, c = place()
    X, Y, C = device(1 - s, z, y, c), device(s, z, 1 - y, c), device(s, z, y, 1 - c)
    z_peers = [device(s, lax.rem(z + d, Z), y, c) for d in range(1, Z)]
    greet(z_peers + [X, Y, C])
    state = {}
    sends = []

    def ship(src, dst, ss, rs, target):
        copy = send(src, dst, ss, rs, target)
        sends.append(copy)
        return copy

    def total(a, b):
        return (a.astype(F32) + b.astype(F32)).astype(BF16)

    def stage0(i):
        own = pltpu.make_async_copy(ins[i].at[:, :, :, c], L0[i], loc.at[i])
        own.start()
        state[i, 0] = (own, ship(ins[i].at[:, :, :, 1 - c], R0[i], cs.at[i], cr.at[i], C))

    def stage1(i):
        own, copy = state[i, 0]
        own.wait()
        copy.wait_recv()
        ka, kb = halves(ins[i].shape[-1])

        def add(t, _):
            at = (t // (Z * 2), (t // 2) % Z, t % 2)
            L0[i][at] = total(L0[i][at], R0[i][at])
            return 0

        lax.fori_loop(0, 4 * Z, add, 0)
        A, B = pl.ds(0, ka), pl.ds(ka, kb)
        state[i, 1] = [ship(L0[i].at[:, :, 1 - y, :, A], R1A[i], ms.at[i, 0], mr.at[i, 0], Y)]
        if kb:
            state[i, 1].append(
                ship(L0[i].at[1 - s, :, :, :, B], R1B[i], ms.at[i, 1], mr.at[i, 1], X)
            )

    def stage2(i):
        for copy in state[i, 1]:
            copy.wait_recv()
        ka, kb = halves(ins[i].shape[-1])
        A, B = slice(0, ka), slice(ka, ka + kb)

        def add(t, _):
            u, zz = t // Z, t % Z
            L0[i][u, zz, y, :, A] = total(L0[i][u, zz, y, :, A], R1A[i][u, zz])
            if kb:
                L0[i][s, zz, u, :, B] = total(L0[i][s, zz, u, :, B], R1B[i][zz, u])
            return 0

        lax.fori_loop(0, 2 * Z, add, 0)
        A, B = pl.ds(0, ka), pl.ds(ka, kb)
        state[i, 2] = [ship(L0[i].at[1 - s, :, y, :, A], R2A[i], ms.at[i, 2], mr.at[i, 2], X)]
        if kb:
            state[i, 2].append(
                ship(L0[i].at[s, :, 1 - y, :, B], R2B[i], ms.at[i, 3], mr.at[i, 3], Y)
            )

    def stage3(i):
        for copy in state[i, 2]:
            copy.wait_recv()
        ka, kb = halves(ins[i].shape[-1])
        A, B = slice(0, ka), slice(ka, ka + kb)

        def add(zz, _):
            L0[i][s, zz, y, :, A] = total(L0[i][s, zz, y, :, A], R2A[i][zz])
            if kb:
                L0[i][s, zz, y, :, B] = total(L0[i][s, zz, y, :, B], R2B[i][zz])
            return 0

        lax.fori_loop(0, Z, add, 0)
        state[i, 3] = [
            ship(
                L0[i].at[s, lax.rem(z + d, Z), y],
                R3[i].at[d - 1],
                zs.at[i, d - 1],
                zr.at[i, d - 1],
                z_peers[d - 1],
            )
            for d in range(1, Z)
        ]

    def stage4(i):
        for copy in state[i, 3]:
            copy.wait_recv()
        acc = L0[i][s, z, y].astype(F32)
        for d in range(1, Z):
            acc = acc + R3[i][d - 1].astype(F32)
        outs[i][...] = acc

    stages = (stage0, stage1, stage2, stage3, stage4)
    for t in range(n + 4):
        for k in range(5):
            if 0 <= t - k < n:
                stages[k](t - k)
    for copy in sends:
        copy.wait_send()


def scatter_all(arrays, Z):
    n = len(arrays)
    D = pltpu.SemaphoreType.DMA

    def buffers(shape_of):
        return [pltpu.VMEM(shape_of(*a.shape[4:]), BF16) for a in arrays]

    def half(columns, k):
        return max(halves(columns)[k], 128)

    return pl.pallas_call(
        functools.partial(scatter_kernel, n, Z),
        out_shape=[jax.ShapeDtypeStruct(a.shape[4:], F32) for a in arrays],
        in_specs=[pl.BlockSpec(memory_space=pl.ANY)] * n,
        out_specs=[pl.BlockSpec(memory_space=pltpu.VMEM)] * n,
        scratch_shapes=buffers(lambda r, k: (2, Z, 2, r, k))
        + buffers(lambda r, k: (2, Z, 2, r, k))
        + buffers(lambda r, k: (2, Z, r, half(k, 0)))
        + buffers(lambda r, k: (Z, 2, r, half(k, 1)))
        + buffers(lambda r, k: (Z, r, half(k, 0)))
        + buffers(lambda r, k: (Z, r, half(k, 1)))
        + buffers(lambda r, k: (Z - 1, r, k))
        + [D((n,)), D((n,)), D((n,)), D((n, 4)), D((n, 4)), D((n, Z - 1)), D((n, Z - 1))],
        compiler_params=pltpu.CompilerParams(
            collective_id=1, has_side_effects=True, vmem_limit_bytes=60 * 2**20
        ),
    )(*arrays)


def head_rows(block, j):
    parts = []
    if j > 0:
        parts.append(jnp.zeros((HD * j, block.shape[1]), block.dtype))
    parts.append(block[HD * j : HD * (j + 1)])
    if j < 3:
        parts.append(jnp.zeros((HD * (3 - j), block.shape[1]), block.dtype))
    return jnp.concatenate(parts, 0)


def head_lanes(block, j):
    lane = lax.broadcasted_iota(jnp.int32, block.shape, 1)
    return jnp.where((lane >= HD * j) & (lane < HD * (j + 1)), block, jnp.zeros_like(block))


def attend_kernel(bias_ref, k_ref, vT_ref, qT_ref, oT_ref, L_ref):
    k = k_ref[...]
    for j in range(4):
        rows = slice(HD * j, HD * (j + 1))
        s = jnp.dot(k, head_rows(qT_ref[...], j), preferred_element_type=F32)
        s = jnp.concatenate([s[:SHORT], s[SHORT:] + bias_ref[...]], 0)
        m = jnp.max(s, axis=0, keepdims=True)
        p = jnp.exp2(s - m)
        total = jnp.sum(p, axis=0, keepdims=True)
        o = jnp.dot(vT_ref[rows, :], p.astype(BF16), preferred_element_type=F32)
        oT_ref[rows, :] = (o * (1.0 / total)).astype(BF16)
        L_ref[0, j : j + 1, :] = m + jnp.log2(total)


def attend(bias, k, vT, qT):
    n, width = k.shape
    tq = n
    groups = width // GROUP
    return pl.pallas_call(
        attend_kernel,
        out_shape=(
            jax.ShapeDtypeStruct((width, n), BF16),
            jax.ShapeDtypeStruct((groups, 4, n), F32),
        ),
        grid=(groups, n // tq),
        in_specs=[
            pl.BlockSpec((n - SHORT, 1), lambda g, i: (0, 0)),
            pl.BlockSpec((n, GROUP), lambda g, i: (0, g)),
            pl.BlockSpec((GROUP, n), lambda g, i: (g, 0)),
            pl.BlockSpec((GROUP, tq), lambda g, i: (g, i)),
        ],
        out_specs=(
            pl.BlockSpec((GROUP, tq), lambda g, i: (g, i)),
            pl.BlockSpec((1, 4, tq), lambda g, i: (g, 0, i)),
        ),
        compiler_params=pltpu.CompilerParams(vmem_limit_bytes=48 * 2**20),
    )(bias, k, vT, qT)


def attend_back_kernel(
    steps,
    bias_ref,
    k_ref,
    kT_ref,
    v_ref,
    qT_ref,
    q_ref,
    goT_ref,
    go_ref,
    oT_ref,
    L_ref,
    gqT_ref,
    gk_ref,
    gv_ref,
    ak,
    av,
):
    i = pl.program_id(1)

    @pl.when(i == 0)
    def _():
        ak[...] = jnp.zeros_like(ak)
        av[...] = jnp.zeros_like(av)

    k = k_ref[...]
    v = v_ref[...]
    for j in range(4):
        rows = slice(HD * j, HD * (j + 1))
        s = jnp.dot(k, head_rows(qT_ref[...], j), preferred_element_type=F32)
        s = jnp.concatenate([s[:SHORT], s[SHORT:] + bias_ref[...]], 0)
        p = jnp.exp2(s - L_ref[0, j : j + 1, :])
        gp = jnp.dot(v, head_rows(goT_ref[...], j), preferred_element_type=F32)
        inner = jnp.sum(
            goT_ref[rows, :].astype(F32) * oT_ref[rows, :].astype(F32), axis=0, keepdims=True
        )
        gs = (p * (gp - inner)).astype(BF16)
        av[...] += jnp.dot(
            p.astype(BF16), head_lanes(go_ref[...], j), preferred_element_type=F32
        )
        ak[...] += jnp.dot(gs, head_lanes(q_ref[...], j), preferred_element_type=F32)
        gq = jnp.dot(kT_ref[rows, :], gs, preferred_element_type=F32)
        gqT_ref[rows, :] = (gq * math.log(2.0)).astype(BF16)

    @pl.when(i == steps - 1)
    def _():
        gk_ref[...] = (ak[...] * HD**-0.5).astype(BF16)
        gv_ref[...] = av[...].astype(BF16)


def attend_back(bias, k, kT, v, qT, q, goT, go, oT, L):
    n, width = k.shape
    tq = n
    groups = width // GROUP
    by_rows = pl.BlockSpec((n, GROUP), lambda g, i: (0, g))
    by_columns = pl.BlockSpec((GROUP, n), lambda g, i: (g, 0))
    query_rows = pl.BlockSpec((tq, GROUP), lambda g, i: (i, g))
    query_columns = pl.BlockSpec((GROUP, tq), lambda g, i: (g, i))
    return pl.pallas_call(
        functools.partial(attend_back_kernel, n // tq),
        out_shape=(
            jax.ShapeDtypeStruct((width, n), BF16),
            jax.ShapeDtypeStruct((n, width), BF16),
            jax.ShapeDtypeStruct((n, width), BF16),
        ),
        grid=(groups, n // tq),
        in_specs=[
            pl.BlockSpec((n - SHORT, 1), lambda g, i: (0, 0)),
            by_rows,
            by_columns,
            by_rows,
            query_columns,
            query_rows,
            query_columns,
            query_rows,
            query_columns,
            pl.BlockSpec((1, 4, tq), lambda g, i: (g, 0, i)),
        ],
        out_specs=(query_columns, by_rows, by_rows),
        scratch_shapes=[pltpu.VMEM((n, GROUP), F32), pltpu.VMEM((n, GROUP), F32)],
        compiler_params=pltpu.CompilerParams(vmem_limit_bytes=48 * 2**20),
    )(bias, k, kT, v, qT, q, goT, go, oT, L)


def mm(spec, a, b):
    return jnp.einsum(spec, a, b, preferred_element_type=F32)


def norm_rows(values, gain, shift):
    center = values - jnp.mean(values, axis=-1, keepdims=True)
    spread = jnp.mean(center * center, axis=-1, keepdims=True)
    return center * lax.rsqrt(spread + NORM_EPS) * (1.0 + gain) + shift


def exact_gelu(values):
    return jax.nn.gelu(values, approximate=False)


def encoder_attend(q, k, v, live):
    heads = lambda m: m.reshape(m.shape[0], HEADS_E, m.shape[1] // HEADS_E)
    scale = (q.shape[1] // HEADS_E) ** -0.5
    s = mm("qhd,khd->hqk", heads(q), heads(k)) * scale
    s = jnp.where(live[None, None, :], s, FAR_BELOW)
    high = jnp.max(s, axis=-1, keepdims=True)
    raised = jnp.exp(s - high)
    p = raised / jnp.sum(raised, axis=-1, keepdims=True)
    o = mm("hqk,khd->qhd", p.astype(BF16), heads(v))
    return o.reshape(q.shape).astype(BF16), p


def encoder_attend_back(kept, go, width):
    q, k, v, p = kept
    heads = lambda m: m.reshape(m.shape[0], HEADS_E, m.shape[1] // HEADS_E)
    scale = (width // HEADS_E) ** -0.5
    g = heads(go)
    gv = mm("hqk,qhd->khd", p.astype(BF16), g)
    gp = mm("qhd,khd->hqk", g, heads(v))
    gs = (p * (gp - jnp.sum(gp * p, axis=-1, keepdims=True))).astype(BF16)
    gq = mm("hqk,khd->qhd", gs, heads(k)) * scale
    gk = mm("hqk,qhd->khd", gs, heads(q)) * scale
    return tuple(m.reshape(q.shape).astype(BF16) for m in (gq, gk, gv))


def decoder_attend(q, k, v, bias):
    scaled = (k * (HD**-0.5 * math.log2(math.e))).astype(BF16)
    q, v = q.astype(BF16), v.astype(BF16)
    oT, L = attend(bias, scaled, v.T, q.T)
    return oT.T, (q, scaled, v, oT, L)


def decoder_attend_back(kept, go, bias):
    q, k, v, oT, L = kept
    gqT, gk, gv = attend_back(bias, k, k.T, v, q.T, q, go.T, go, oT, L)
    return gqT.T, gk, gv


def block_forward(inputs, live, weights, encoder):
    gains, qkv, proj, fc1, fc1_bias, fc2 = weights
    width = inputs.shape[1]
    normed = norm_rows(inputs, gains[0], gains[1]).astype(BF16)
    joined = mm("rd,de->re", normed, qkv)
    q = joined[:, :width] + gains[4]
    k = joined[:, width : 2 * width]
    v = joined[:, 2 * width :] + gains[5]
    if encoder:
        q, k, v = (m.astype(BF16) for m in (q, k, v))
        attended, p = encoder_attend(q, k, v, live)
        kept_attend = (q, k, v, p)
    else:
        attended, kept_attend = decoder_attend(q, k, v, live)
    middle = inputs + (mm("rd,de->re", attended, proj) + gains[6])
    normed_two = norm_rows(middle, gains[2], gains[3]).astype(BF16)
    hidden = mm("rd,df->rf", normed_two, fc1) + fc1_bias
    active = exact_gelu(hidden).astype(BF16)
    result = middle + (mm("rf,fd->rd", active, fc2) + gains[7])
    return result, (inputs, normed, kept_attend, attended, middle, normed_two, hidden, active)


def block_backward(grad_out, kept, weights, bias, encoder):
    gains, qkv, proj, fc1, fc1_bias, fc2 = weights
    inputs, normed, kept_attend, attended, middle, normed_two, hidden, active = kept
    gy = grad_out.astype(BF16)
    g_fc2 = mm("rf,rd->fd", active, gy).astype(BF16)
    unused, gelu_pull = jax.vjp(exact_gelu, hidden)
    gz = gelu_pull(mm("rd,fd->rf", gy, fc2))[0].astype(BF16)
    g_fc1 = mm("rd,rf->df", normed_two, gz).astype(BF16)
    unused, second_pull = jax.vjp(norm_rows, middle, gains[2], gains[3])
    g_middle, g2, g3 = second_pull(mm("rf,df->rd", gz, fc1))
    g_middle = g_middle + grad_out
    ga = g_middle.astype(BF16)
    g_proj = mm("rd,re->de", attended, ga).astype(BF16)
    go = mm("re,de->rd", ga, proj).astype(BF16)
    if encoder:
        gq, gk, gv = encoder_attend_back(kept_attend, go, inputs.shape[1])
    else:
        gq, gk, gv = decoder_attend_back(kept_attend, go, bias)
    joined = jnp.concatenate([gq, gk, gv], axis=1)
    g_qkv = mm("rd,re->de", normed, joined).astype(BF16)
    unused, first_pull = jax.vjp(norm_rows, inputs, gains[0], gains[1])
    g_inputs, g0, g1 = first_pull(mm("re,de->rd", joined, qkv))
    g_inputs = g_inputs + g_middle
    rows = [jnp.sum(m.astype(F32), 0) for m in (gq, gv, ga, gy)]
    g_vectors = jnp.stack([g0, g1, g2, g3] + rows)
    return g_inputs, (g_vectors, g_qkv, g_proj, g_fc1, jnp.sum(gz.astype(F32), 0), g_fc2)


SMALL = 2048


def body(
    patches,
    lengths,
    keep_order,
    e_vectors,
    e_qkv,
    e_proj,
    e_fc1,
    e_fc1_bias,
    e_fc2,
    embed,
    d_vectors,
    dec_pos,
    d_qkv,
    d_proj,
    d_fc1,
    d_fc1_bias,
    d_fc2,
    cotangent,
):
    count = lax.axis_size("segment") * lax.axis_size("dp")
    Z = lax.axis_size("dp") // 4
    device_index = lax.axis_index(AXES)
    small_shards = (e_vectors, e_fc1_bias, d_vectors, d_fc1_bias)
    sizes = [m.size for m in small_shards]
    small = jnp.concatenate([m.reshape(-1) for m in small_shards])
    small = jnp.pad(small, (0, SMALL - small.size)).reshape(SMALL // 128, 128)
    sent = (small, e_qkv, e_proj, e_fc1, e_fc2, embed, dec_pos.T, d_qkv, d_proj, d_fc1, d_fc2)
    full = gather_all([m.astype(BF16) for m in sent], Z)
    small_all = full[0].reshape(count, SMALL).astype(F32)
    parts, start = [], 0
    for size in sizes:
        parts.append(small_all[:, start : start + size])
        start += size

    def by_columns(part, rows):
        return part.reshape(count, rows, -1).transpose(1, 0, 2).reshape(rows, -1)

    e_gains, d_gains = by_columns(parts[0], 8), by_columns(parts[2], 10)
    mats = [m.reshape(-1, m.shape[-1]) for m in full[1:]]
    w_qkv, w_proj, w_fc1, w_fc2, w_embed, posT, dw_qkv, dw_proj, dw_fc1, dw_fc2 = mats
    enc = (e_gains, w_qkv, w_proj, w_fc1, parts[1].reshape(-1), w_fc2)
    dec = (d_gains, dw_qkv, dw_proj, dw_fc1, parts[3].reshape(-1), dw_fc2)

    def run_cube(patch, cotan, length, order):
        slots = patch.shape[0]
        keep = jnp.arange(VIS) < length // 10
        places = order[:VIS]
        spots = jnp.where(keep, places, slots)
        rows_in = jnp.where(keep[:, None], jnp.take(patch, places, axis=0).astype(F32), 0.0)
        encoded, kept_e = block_forward(rows_in, keep, enc, True)
        encoded = encoded.astype(BF16)
        embedded = mm("rd,de->re", encoded, w_embed) + d_gains[8]
        filled = jnp.broadcast_to(d_gains[9], (slots, d_gains.shape[1]))
        filled = filled.at[spots].set(embedded, mode="drop")
        inputs = filled + posT.T.astype(F32)
        live = (jnp.arange(slots) < length)[:, None]
        bias = jnp.where(live[SHORT:], 0.0, FAR_BELOW).astype(F32)
        result, kept_d = block_forward(inputs, bias, dec, False)
        decoded = jnp.where(live, result, 0.0).astype(BF16)
        G = jnp.where(live, cotan.astype(F32), 0.0)
        gxd, dg = block_backward(G, kept_d, dec, bias, False)
        picked = jnp.where(keep[:, None], jnp.take(gxd, places, axis=0), 0.0)
        gemb = picked.astype(BF16)
        g_embed = mm("rd,re->de", encoded, gemb).astype(BF16)
        gencoded = mm("re,de->rd", gemb, w_embed).astype(BF16)
        g_token = jnp.sum(gxd, 0) - jnp.sum(picked, 0)
        d_vec = jnp.concatenate(
            [dg[0], jnp.stack([jnp.sum(gemb.astype(F32), 0), g_token])], 0
        )
        g_rows, eg = block_backward(gencoded.astype(F32), kept_e, enc, None, True)
        g_patch = jnp.zeros((slots, patch.shape[1]), F32).at[spots].set(g_rows, mode="drop")
        return decoded, g_patch, eg, g_embed, d_vec, gxd.T.astype(BF16), dg

    own = patches.shape[0]
    base = device_index * own
    runs = [
        run_cube(patches[i], cotangent[i], lengths[base + i], keep_order[base + i])
        for i in range(own)
    ]
    decoded = jnp.stack([r[0] for r in runs])
    patches_grad = jnp.stack([r[1] for r in runs])
    eg, g_embed, d_vec, g_pos, dg = jax.tree.map(
        lambda *m: functools.reduce(lambda a, b: a + b, m), *[r[2:] for r in runs]
    )

    def to_devices(vector, rows):
        return vector.reshape(rows, count, -1).transpose(1, 0, 2).reshape(count, -1)

    g_small = jnp.concatenate(
        [
            to_devices(eg[0], 8),
            eg[4].reshape(count, -1),
            to_devices(d_vec, 10),
            dg[4].reshape(count, -1),
        ],
        axis=1,
    )
    g_small = jnp.pad(g_small, ((0, 0), (0, SMALL - g_small.shape[1])))
    g_small = g_small.reshape(count, SMALL // 128, 128).astype(BF16)

    def blocks(m):
        return m.reshape((2, Z, 2, 2, -1, m.shape[-1]))

    order = (dg[5], dg[3], dg[2], dg[1], g_pos, g_embed, eg[5], eg[3], eg[2], eg[1], g_small)
    out = scatter_all([blocks(m) for m in order], Z)
    dr_fc2, dr_fc1, dr_proj, dr_qkv, r_pos, r_embed, r_fc2, r_fc1, r_proj, r_qkv, r_small = out
    flat = r_small.reshape(-1)
    parts, start = [], 0
    for shard in small_shards:
        parts.append(flat[start : start + shard.size].reshape(shard.shape))
        start += shard.size
    return (
        decoded,
        patches_grad,
        parts[0],
        r_qkv,
        r_proj,
        r_fc1,
        parts[1],
        r_fc2,
        r_embed,
        parts[2],
        r_pos.T,
        dr_qkv,
        dr_proj,
        dr_fc1,
        parts[3],
        dr_fc2,
    )


def solution(mesh):
    rows, columns, cubes = P(AXES, None), P(None, AXES), P(AXES, None, None)
    weights = (columns, rows, rows, rows, P(AXES), rows, rows, columns, columns)
    weights = weights + (rows, rows, rows, P(AXES), rows)
    return jax.shard_map(
        body,
        mesh=mesh,
        in_specs=(cubes, P(), P()) + weights + (cubes,),
        out_specs=(cubes, cubes) + weights,
        check_vma=False,
    )
```

time: 2810 us -> 526 us (0.19)
  waiting for transfers between devices: 2240 us -> 0 us
  Pallas kernels: 0 us -> 302 us
  blocking collectives: 256 us -> 0 us
  other arithmetic: 99.2 us -> 42.6 us
    reduce_scatter x10 -> x0, waiting for transfers between devices: 1160 us -> none  [the longest x1 143 us: share_each(): lax.psum_scatter(grads[11], ('segment', 'dp'), scatter_dimension=0, tiled...]
    ppermute x7 -> x0, waiting for transfers between devices: 861 us -> none  [shifted(): lax.ppermute(value, axis, [(source, source + steps) for source in range(f...]
    pallas_call x0 -> x4, Pallas kernels: none -> 302 us  [the longest x1 118 us: scatter_all(): pl.pallas_call(functools.partial(scatter_kernel, n, Z), out_shape=[jax.Sh...]
    all_gather x8 -> x0, waiting for transfers between devices: 221 us -> none  [the longest x1 65.8 us: body(): lax.all_gather(e_fc2.astype(jnp.bfloat16), ('segment', 'dp'), axis=0, til...]
    all_gather x4 -> x0, blocking collectives: 164 us -> none  [the longest x1 44.3 us: body(): lax.all_gather(d_proj.astype(jnp.bfloat16), ('segment', 'dp'), axis=0, ti...]
    unnamed x2 -> x0, blocking collectives: 92.2 us -> none
    add x20 -> x0, other arithmetic: 67.3 us -> none  [the longest x14 67.1 us: body(): before + added]
    another operation x30 -> x9, local copies, waits for them, and re-layouts: 29.4 us -> 0.77 us  [block_backward(): g_vectors = jnp.stack([g0, g1, g2, g3] + rows)]
  transfers between devices with their start and end apart: 26 -> 0, of which waited for: 15 -> 0; matrix products, arithmetic and copies ran while one was open for 7% -> 0% of each run, Pallas kernels for 0% -> 0%
where the time goes in v1:
time: 526 us; the launch traced here: 516 us
  Pallas kernels  302 us (57%)
  matrix products  106 us (20%)
  local copies, waits for them, and re-layouts  61.3 us (12%)
  other arithmetic  42.6 us (8%)
    pallas_call x1, Pallas kernels, scatter_all(): pl.pallas_call(functools.partial(scatter_kernel, n, Z), out_shape=[jax.Sh...  118 us
    pallas_call x1, Pallas kernels, gather_all(): pl.pallas_call(functools.partial(gather_kernel, n, Z), out_shape=[jax.Sha...  118 us
    dot_general x32, matrix products, mm(): return jnp.einsum(spec, a, b, preferred_element_type=F32)  105 us
    pallas_call x1, Pallas kernels, attend_back(): pl.pallas_call(functools.partial(attend_back_kernel, n // tq), out_shape=...  43.1 us
    unnamed x186, local copies, waits for them, and re-layouts  31.4 us
    pallas_call x1, Pallas kernels, attend(): pl.pallas_call(attend_kernel, out_shape=(jax.ShapeDtypeStruct((width, n),...  22.7 us
    convert_element_type x11, other arithmetic, body(): full = gather_all([m.astype(BF16) for m in sent], Z)  15.9 us

profile of v1, /device:TPU:0, one launch (start us, length us, event | category | flops | bytes accessed | tf_op | source)
XLA Modules:
  0.0 516.4 jit_solution(9355528696685585572)
XLA Ops:
  27.7 118.0 %shard_map.297 = (bf16[2,4,2,2,16,128]{5,4,3,2,1,0:T(8,128)(2,1)}, bf16[2,4,2,2,24,2304]{5,4,3,2,1,0:T(8,128)(2,1)}, bf16[2,4,2,2,24,768]{5,4,3,2,1,0:T(8,128)(2...) custom-call(bf16[16,128]{1,0:T(8,128)(2,1)} %fusion.71.refs_0_, ...), custom_call_target="tpu_custom_call" | custom-call | tf_op jit(solution)/shard_map/pallas_call | solution.py:134
  150.1 2.8 fusion.87
  156.4 7.4 %multiply_convert_fusion.2 = (bf16[104,3072]{1,0:T(8,128)(2,1)S(1)}, f32[104,3072]{1,0:T(8,128)}, f32[104,3072]{1,0:T(8,128)}) fusion(f32[3072]{0:T(1024)S(1)} %add.336, bf16[768,3072]{1,0:T(8,128)(2,1)} %bitcast.181, f32[104,768]{1,0:T(8,128)S(1)} %get-tuple-element.167, f32[768]{0:T(1024)S(1)} %add.333, f32[768]{0:T(1024)S(1)} %add.332, ...), kind=kOutput, calls=%fused_computation.68 | convolution fusion | flops 512219136 | bytes 8252224 | tf_op jit(solution)/shard_map/rd,df->rf/dot_general | solution.py:425
  165.7 2.2 scatter_fusion
  169.7 2.0 fusion.104
  173.8 2.0 fusion.89
  175.9 2.2 fusion.11
  178.1 3.7 copy.101
  189.9 22.7 %shard_map.298 = (bf16[512,1024]{1,0:T(8,128)(2,1)S(1)}, f32[4,4,1024]{2,1,0:T(4,128)S(1)}) custom-call(f32[448,1]{1,0:T(8,128)S(1)} %copy.71.bias_ref, bf16[1024,512]{1,0:T(8,128)(2,1)S(1)} %copy.72.k_ref, bf16[512,1024]{1,0:T(8,128)(2,1)S(1)} %copy-done.3, bf16[512,1024]{1,0:T(8,128)(2,1)S(1)} %copy.74.qT_ref), custom_call_target="tpu_custom_call" | custom-call | tf_op jit(solution)/shard_map/pallas_call | solution.py:319
  214.0 2.0 copy-done.71
  216.1 22.3 %multiply_convert_fusion = (bf16[1024,2048]{1,0:T(8,128)(2,1)S(1)}, f32[1024,2048]{1,0:T(8,128)S(1)}, f32[1024,2048]{1,0:T(8,128)}) fusion(f32[2048]{0:T(1024)S(1)} %add.369, bf16[512,2048]{1,0:T(8,128)(2,1)S(1)} %bitcast.238, f32[1024,512]{0,1:T(8,128)S(1)} %get-tuple-element.170, f32[512]{0:T(512)S(1)} %add.366, f32[512]{0:T(512)S(1)} %add.365, ...), kind=kOutput, calls=%fused_computation.8 | convolution fusion | flops 2288517120 | bytes 25186304 | tf_op jit(solution)/shard_map/rd,df->rf/dot_general | solution.py:425
  238.4 9.0 %fusion.111 = (bf16[2048]{0:T(1024)(128)(2,1)S(1)}, bf16[1024,2048]{1,0:T(8,128)(2,1)}) fusion(f32[1024,2048]{1,0:T(8,128)S(1)} %get-tuple-element.140, bf16[2048,512]{1,0:T(8,128)(2,1)S(1)} %bitcast.239, bf16[1,1024,512]{1,2,0:T(8,128)(2,1)S(1)} %copy-done.21, pred[1024]{0:T(1024)(128)(4,1)S(1)} %iota_compare_fusion.2, ...), kind=kOutput, calls=%fused_computation.250 | convolution fusion | flops 2182608896 | bytes 24130560 | tf_op jit(solution)/shard_map/rd,fd->rf/dot_general | solution.py:425
  247.4 3.4 fusion.16
  250.8 3.8 convolution_convert_fusion.4
  254.6 2.5 copy.94
  257.2 6.4 %multiply_reduce_fusion = (bf16[512]{0:T(512)(128)(2,1)S(1)}, f32[1024]{0:T(1024)S(1)}, bf16[512]{0:T(512)(128)(2,1)S(1)}, f32[1024,512]{0,1:T(8,128)S(1)}) fusion(f32[1024,512]{0,1:T(8,128)} %copy-done.13, f32[1024]{0:T(1024)S(1)} %fusion.73, f32[1024]{0:T(1024)S(1)} %broadcast_multiply_fusion, f32[512]{0:T(512)S(1)} %add.365, ...), kind=kOutput, calls=%fused_computation.44 | convolution fusion | flops 2151675904 | bytes 10502144 | tf_op jit(solution)/shard_map/rf,df->rd/dot_general | solution.py:425
  263.6 3.9 convolution_convert_fusion.3
  269.6 3.0 fusion.98
  272.7 3.2 convolution_convert_fusion.7.go_ref
  277.5 2.3 copy.84.goT_ref
  279.8 43.1 %shard_map.299 = (bf16[512,1024]{1,0:T(8,128)(2,1)S(1)}, bf16[1024,512]{1,0:T(8,128)(2,1)S(1)}, bf16[1024,512]{1,0:T(8,128)(2,1)S(1)}) custom-call(f32[448,1]{1,0:T(8,128)S(1)} %copy.71.bias_ref, bf16[1024,512]{1,0:T(8,128)(2,1)S(1)} %copy.72.k_ref, bf16[512,1024]{1,0:T(8,128)(2,1)S(1)} %fusion.168.kT_ref, bf16[1024,512]{1,0:T(8,128)(2,1)} %copy-done.20, ...), custom_call_target="tpu_custom_call" | custom-call | tf_op jit(solution)/shard_map/pallas_call | solution.py:398
  327.1 4.5 fusion.91
  331.6 3.1 convolution_convert_fusion.5
  341.2 2.6 gather_fusion.1
  344.4 4.8 fusion.94
  349.2 4.1 multiply_reduce_fusion.7
  356.1 2.2 fusion.113
  366.8 3.1 scatter_custom_fusion.1
  370.0 3.1 convolution_convert_fusion
  373.0 3.6 convolution_convert_fusion.1
  376.7 3.6 convolution_convert_fusion.2
  380.3 118.5 %shard_map.300 = (f32[64,512]{1,0:T(8,128)}, f32[16,2048]{1,0:T(8,128)}, f32[16,512]{1,0:T(8,128)}, f32[16,1536]{1,0:T(8,128)}, f32[16,1024]{1,0:T(8,128)}, /*in...) custom-call(bf16[2,4,2,2,64,512]{5,4,3,2,1,0:T(8,128)(2,1)} %bitcast, ...), custom_call_target="tpu_custom_call" | custom-call | tf_op jit(solution)/shard_map/pallas_call | solution.py:267
  (343 shorter events, 91.2 us)
Async XLA Ops:
  0.7 25.7 %copy-start.35 = (bf16[1,1024,512]{2,1,0:T(8,128)(2,1)S(1)}, bf16[1,1024,512]{2,1,0:T(8,128)(2,1)}, u32[]{:S(2)}) copy-start(bf16[1,1024,512]{2,1,0:T(8,128)(2,1)} %param.35) | copy-start | bytes 3145732
  8.3 19.5 %copy-start.66 = (s32[1024]{0:T(1024)}, s32[1024]{0:T(1024)S(1)}, u32[]{:S(2)}) copy-start(s32[1024]{0:T(1024)S(1)} %pad_clamp_fusion) | copy-start | bytes 12292
  25.8 129.6 %copy-start.23 = (bf16[104,768]{1,0:T(8,128)(2,1)}, bf16[104,768]{1,0:T(8,128)(2,1)S(1)}, u32[]{:S(2)}) copy-start(bf16[104,768]{1,0:T(8,128)(2,1)S(1)} %gather_fusion) | copy-start | bytes 479236
  26.0 124.0 %copy-start.60 = (f32[104]{0:T(128)}, f32[104]{0:T(128)S(1)}, u32[]{:S(2)}) copy-start(f32[104]{0:T(128)S(1)} %broadcast_multiply_fusion.3) | copy-start | bytes 1252
  26.2 121.7 %copy-start.67 = (f32[104]{0:T(128)}, f32[104]{0:T(128)S(1)}, u32[]{:S(2)}) copy-start(f32[104]{0:T(128)S(1)} %multiply_reduce_fusion.12) | copy-start | bytes 1252
  26.2 123.8 %copy-start.64 = (f32[104]{0:T(128)}, f32[104]{0:T(128)S(1)}, u32[]{:S(2)}) copy-start(f32[104]{0:T(128)S(1)} %fusion.76) | copy-start | bytes 1252
  149.6 6.8 %copy-start.56 = (f32[768]{0:T(1024)}, f32[768]{0:T(1024)S(1)}, u32[]{:S(2)}) copy-start(f32[768]{0:T(1024)S(1)} %add.333) | copy-start | bytes 9220
  155.9 7.9 %copy-start.17 = (f32[104,768]{1,0:T(8,128)}, f32[104,768]{1,0:T(8,128)S(1)}, u32[]{:S(2)}) copy-start(f32[104,768]{1,0:T(8,128)S(1)} %get-tuple-element.167) | copy-start | bytes 958468
  156.1 7.7 %copy-start.69 = (f32[104]{0:T(128)}, f32[104]{0:T(128)S(1)}, u32[]{:S(2)}) copy-start(f32[104]{0:T(128)S(1)} %multiply_reduce_fusion.11) | copy-start | bytes 1252
  156.1 7.7 %slice-start = ((s8[4718592]{0:T(1024)(128)(4,1)}), s8[4194304]{0:T(1024)(128)(4,1)S(1)}, s32[]{:S(2)}) async-start(s8[4718592]{0:T(1024)(128)(4,1)} %bitcast.178), calls=%async_computation | async-start | bytes 8388608
  156.4 7.4 %slice-start.1 = ((s8[4718592]{0:T(1024)(128)(4,1)}), s8[524288]{0:T(1024)(128)(4,1)S(1)}, s32[]{:S(2)}) async-start(s8[4718592]{0:T(1024)(128)(4,1)} %bitcast.178), calls=%async_computation.1 | async-start | bytes 1048576
  178.1 3.7 copy-start.19
  178.1 4.2 copy-start.20
  182.4 6.3 %copy-start.2 = (bf16[512,1024]{1,0:T(8,128)(2,1)}, bf16[512,1024]{1,0:T(8,128)(2,1)S(1)}, u32[]{:S(2)}) copy-start(bf16[512,1024]{1,0:T(8,128)(2,1)S(1)} %copy.74.qT_ref) | copy-start | bytes 3145732
  189.9 22.7 %copy-start.11 = (f32[1024,512]{0,1:T(8,128)S(1)}, f32[1024,512]{0,1:T(8,128)}, u32[]{:S(2)}) copy-start(f32[1024,512]{0,1:T(8,128)} %copy-done.10) | copy-start | bytes 6291460
  189.9 22.7 %copy-start.45 = (bf16[2,4,2,2,16,512]{5,4,3,2,1,0:T(8,128)(2,1)S(1)}, bf16[2,4,2,2,16,512]{5,4,3,2,1,0:T(8,128)(2,1)}, u32[]{:S(2)}) copy-start(bf16[2,4,2,2,16,512]{5,4,3,2,1,0:T(8,128)(2,1)} %get-tuple-element.52) | copy-start | bytes 1572868
  213.7 33.7 %copy-start.13 = (f32[1024,512]{0,1:T(8,128)}, f32[1024,512]{0,1:T(8,128)S(1)}, u32[]{:S(2)}) copy-start(f32[1024,512]{0,1:T(8,128)S(1)} %get-tuple-element.170) | copy-start | bytes 6291460
  216.0 22.3 %copy-start.21 = (bf16[1,1024,512]{1,2,0:T(8,128)(2,1)S(1)}, bf16[1,1024,512]{1,2,0:T(8,128)(2,1)}, u32[]{:S(2)}) copy-start(bf16[1,1024,512]{1,2,0:T(8,128)(2,1)} %copy.80) | copy-start | bytes 3145732
  216.1 22.3 %copy-start.72 = (bf16[2,4,2,2,64,512]{5,4,3,2,1,0:T(8,128)(2,1)S(1)}, bf16[2,4,2,2,64,512]{5,4,3,2,1,0:T(8,128)(2,1)}, u32[]{:S(2)}) copy-start(bf16[2,4,2,2,64,512]{5,4,3,2,1,0:T(8,128)(2,1)} %get-tuple-element.54) | copy-start | bytes 6291460
  257.2 6.4 %copy-start.14 = (f32[1024,512]{0,1:T(8,128)S(1)}, f32[1024,512]{0,1:T(8,128)}, u32[]{:S(2)}) copy-start(f32[1024,512]{0,1:T(8,128)} %copy-done.13) | copy-start | bytes 6291460
  257.2 6.4 %copy-start.74 = (bf16[1024,2048]{1,0:T(8,128)(2,1)S(1)}, bf16[1024,2048]{1,0:T(8,128)(2,1)}, u32[]{:S(2)}) copy-start(bf16[1024,2048]{1,0:T(8,128)(2,1)} %get-tuple-element.179) | copy-start | bytes 12582916
  272.6 3.4 copy-start.5
  327.1 4.5 copy-start.12
  327.1 4.5 copy-start.36
  344.4 4.8 copy-start.18
  349.2 4.1 copy-start.70
  373.0 3.7 copy-start.26
  380.3 135.9 %copy-start.1 = (bf16[1,1024,768]{2,1,0:T(8,128)(2,1)S(1)}, bf16[1,1024,768]{2,1,0:T(8,128)(2,1)}, u32[]{:S(2)}) copy-start(bf16[1,1024,768]{2,1,0:T(8,128)(2,1)} %param.18) | copy-start | bytes 4718596
  498.8 14.8 %copy-start.58 = (f32[16,1536]{1,0:T(8,128)S(1)}, f32[16,1536]{1,0:T(8,128)}, u32[]{:S(2)}) copy-start(f32[16,1536]{1,0:T(8,128)} %get-tuple-element.213) | copy-start | bytes 294916
  498.8 15.4 %copy-start.59 = (f32[16,512]{1,0:T(8,128)S(1)}, f32[16,512]{1,0:T(8,128)}, u32[]{:S(2)}) copy-start(f32[16,512]{1,0:T(8,128)} %get-tuple-element.214) | copy-start | bytes 98308
  498.8 16.0 %copy-start.55 = (f32[16,2048]{1,0:T(8,128)S(1)}, f32[16,2048]{1,0:T(8,128)}, u32[]{:S(2)}) copy-start(f32[16,2048]{1,0:T(8,128)} %get-tuple-element.215) | copy-start | bytes 393220
  498.8 16.7 %copy-start.54 = (f32[64,512]{1,0:T(8,128)S(1)}, f32[64,512]{1,0:T(8,128)}, u32[]{:S(2)}) copy-start(f32[64,512]{1,0:T(8,128)} %get-tuple-element.217) | copy-start | bytes 393220
  (45 other events, 88.5 us)

commit v2 on v1

v2 whole, which is shorter than its diff:
```python
import functools
import math

import jax
import jax.numpy as jnp
from jax import lax
from jax.experimental import pallas as pl
from jax.experimental.pallas import tpu as pltpu
from jax.sharding import PartitionSpec as P

HEADS_E = 12
HEADS_D = 16
VIS = 104
SHORT = 576
HD = 32
GROUP = 128
F32 = jnp.float32
BF16 = jnp.bfloat16
AXES = ("segment", "dp")
MESH = pl.DeviceIdType.MESH
ROWS_E = 128
NORM_EPS = 1e-06
FAR_BELOW = -1e30


SMALL_ROWS = 32
POS_AT = 5


def place():
    s = lax.axis_index("segment")
    dp = lax.axis_index("dp")
    return s, dp // 4, (dp // 2) % 2, dp % 2


def device(s, z, y, c):
    return (s, (z * 2 + y) * 2 + c)


def halves(columns):
    return (columns // 2, columns // 2) if columns % 256 == 0 else (columns, 0)


def greet(peers):
    barrier = pltpu.get_barrier_semaphore()
    for peer in peers:
        pl.semaphore_signal(barrier, inc=1, device_id=peer, device_id_type=MESH)
    pl.semaphore_wait(barrier, len(peers))


def send(src, dst, send_sem, recv_sem, target):
    copy = pltpu.make_async_remote_copy(
        src_ref=src,
        dst_ref=dst,
        send_sem=send_sem,
        recv_sem=recv_sem,
        device_id=target,
        device_id_type=MESH,
    )
    copy.start()
    return copy


def gather_kernel(n, Z, *refs):
    m = n + 3
    given, outs, ins, shards = refs[:m], refs[m : m + n], refs[m + n : m + 2 * n], refs[m + 2 * n : 2 * m + 2 * n]
    get, loc, zs, zr, ms, mr, cs, cr = refs[2 * m + 2 * n :]
    loads = [pltpu.make_async_copy(given[i], shards[i], get.at[i]) for i in range(m)]
    for load in loads:
        load.start()

    def cast(i):
        if i == 0:
            small = ins[0]
            small[...] = jnp.zeros_like(small)
            for row, k in zip((0, 8, 24, 25), range(4)):
                loads[k].wait()
                ref = shards[k]
                small[row : row + ref.shape[0], : ref.shape[1]] = ref[...].astype(BF16)
        else:
            loads[i + 3].wait()
            ref = shards[i + 3]
            ins[i][...] = (ref[...].T if i == 1 + POS_AT else ref[...]).astype(BF16)

    s, z, y, c = place()
    X, Y, C = device(1 - s, z, y, c), device(s, z, 1 - y, c), device(s, z, y, 1 - c)
    z_peers = [device(s, lax.rem(z + d, Z), y, c) for d in range(1, Z)]
    greet(z_peers + [X, Y, C])
    state = {}
    sends = []

    def both(ref, i, sems, k, target):
        copy = send(ref, ref, sems[0].at[i, k], sems[1].at[i, k], target)
        sends.append(copy)
        return copy

    def stage0(i):
        cast(i)
        own = pltpu.make_async_copy(ins[i], outs[i].at[s, z, y, c], loc.at[i])
        own.start()
        copies = [
            send(ins[i], outs[i].at[s, z, y, c], zs.at[i, d], zr.at[i, d], z_peers[d])
            for d in range(Z - 1)
        ]
        sends.extend(copies)
        state[i, 0] = (own, copies)

    def stage1(i):
        own, copies = state[i, 0]
        own.wait()
        for copy in copies:
            copy.wait_recv()
        o = outs[i]
        ka, kb = halves(o.shape[-1])
        A, B = pl.ds(0, ka), pl.ds(ka, kb)
        state[i, 1] = [both(o.at[s, :, y, c, :, A], i, (ms, mr), 0, X)]
        if kb:
            state[i, 1].append(both(o.at[s, :, y, c, :, B], i, (ms, mr), 1, Y))
        state[i, 9] = [both(o.at[s, :, y, c], i, (cs, cr), 0, C)]

    def stage2(i):
        for copy in state[i, 1]:
            copy.wait_recv()
        o = outs[i]
        ka, kb = halves(o.shape[-1])
        A, B = pl.ds(0, ka), pl.ds(ka, kb)
        state[i, 2] = [both(o.at[:, :, y, c, :, A], i, (ms, mr), 2, Y)]
        state[i, 9].append(both(o.at[1 - s, :, y, c, :, A], i, (cs, cr), 1, C))
        if kb:
            state[i, 2].append(both(o.at[s, :, :, c, :, B], i, (ms, mr), 3, X))
            state[i, 9].append(both(o.at[s, :, 1 - y, c, :, B], i, (cs, cr), 2, C))

    def stage3(i):
        for copy in state[i, 2]:
            copy.wait_recv()
        o = outs[i]
        ka, kb = halves(o.shape[-1])
        A, B = pl.ds(0, ka), pl.ds(ka, kb)
        state[i, 9].append(both(o.at[:, :, 1 - y, c, :, A], i, (cs, cr), 3, C))
        if kb:
            state[i, 9].append(both(o.at[1 - s, :, :, c, :, B], i, (cs, cr), 4, C))

    stages = (stage0, stage1, stage2, stage3)
    for t in range(n + 3):
        for k in range(4):
            if 0 <= t - k < n:
                stages[k](t - k)
    for i in range(n):
        for copy in state[i, 9]:
            copy.wait_recv()
    for copy in sends:
        copy.wait_send()


def gather_all(small_shards, arrays, Z):
    shapes = [(SMALL_ROWS, 128)] + [a.shape for a in arrays]
    shapes[1 + POS_AT] = shapes[1 + POS_AT][::-1]
    n = len(shapes)
    D = pltpu.SemaphoreType.DMA
    return pl.pallas_call(
        functools.partial(gather_kernel, n, Z),
        out_shape=[jax.ShapeDtypeStruct((2, Z, 2, 2) + s, BF16) for s in shapes],
        in_specs=[pl.BlockSpec(memory_space=pl.ANY)] * (n + 3),
        out_specs=[pl.BlockSpec(memory_space=pl.ANY)] * n,
        scratch_shapes=[pltpu.VMEM(s, BF16) for s in shapes]
        + [pltpu.VMEM(a.shape, F32) for a in (*small_shards, *arrays)]
        + [
            D((n + 3,)),
            D((n,)),
            D((n, Z - 1)),
            D((n, Z - 1)),
            D((n, 4)),
            D((n, 4)),
            D((n, 5)),
            D((n, 5)),
        ],
        compiler_params=pltpu.CompilerParams(
            collective_id=0, has_side_effects=True, vmem_limit_bytes=60 * 2**20
        ),
    )(*small_shards, *arrays)


def scatter_kernel(n, Z, *refs):
    ins, outs = refs[:n], refs[n : 2 * n]
    L0, R0, R1A, R1B, R2A, R2B = [refs[(2 + i) * n : (3 + i) * n] for i in range(6)]
    loc, cs, cr, ms, mr, zs, zr = refs[8 * n :]
    s, z, y, c = place()
    X, Y, C = device(1 - s, z, y, c), device(s, z, 1 - y, c), device(s, z, y, 1 - c)
    z_peers = [device(s, lax.rem(z + d, Z), y, c) for d in range(1, Z)]
    greet(z_peers + [X, Y, C])
    state = {}
    sends = []

    def ship(src, dst, ss, rs, target):
        copy = send(src, dst, ss, rs, target)
        sends.append(copy)
        return copy

    def total(a, b):
        return (a.astype(F32) + b.astype(F32)).astype(BF16)

    def stage0(i):
        own = pltpu.make_async_copy(ins[i].at[:, :, :, c], L0[i], loc.at[i])
        own.start()
        state[i, 0] = (own, ship(ins[i].at[:, :, :, 1 - c], R0[i], cs.at[i], cr.at[i], C))

    def stage1(i):
        own, copy = state[i, 0]
        own.wait()
        copy.wait_recv()
        ka, kb = halves(ins[i].shape[-1])

        def add(t, _):
            at = (t // (Z * 2), (t // 2) % Z, t % 2)
            L0[i][at] = total(L0[i][at], R0[i][at])
            return 0

        lax.fori_loop(0, 4 * Z, add, 0)
        A, B = pl.ds(0, ka), pl.ds(ka, kb)
        state[i, 1] = [ship(L0[i].at[:, :, 1 - y, :, A], R1A[i], ms.at[i, 0], mr.at[i, 0], Y)]
        if kb:
            state[i, 1].append(
                ship(L0[i].at[1 - s, :, :, :, B], R1B[i], ms.at[i, 1], mr.at[i, 1], X)
            )

    def stage2(i):
        for copy in state[i, 1]:
            copy.wait_recv()
        ka, kb = halves(ins[i].shape[-1])
        A, B = slice(0, ka), slice(ka, ka + kb)

        def add(t, _):
            u, zz = t // Z, t % Z
            L0[i][u, zz, y, :, A] = total(L0[i][u, zz, y, :, A], R1A[i][u, zz])
            if kb:
                L0[i][s, zz, u, :, B] = total(L0[i][s, zz, u, :, B], R1B[i][zz, u])
            return 0

        lax.fori_loop(0, 2 * Z, add, 0)
        A, B = pl.ds(0, ka), pl.ds(ka, kb)
        state[i, 2] = [ship(L0[i].at[1 - s, :, y, :, A], R2A[i], ms.at[i, 2], mr.at[i, 2], X)]
        if kb:
            state[i, 2].append(
                ship(L0[i].at[s, :, 1 - y, :, B], R2B[i], ms.at[i, 3], mr.at[i, 3], Y)
            )

    def stage3(i):
        for copy in state[i, 2]:
            copy.wait_recv()
        ka, kb = halves(ins[i].shape[-1])
        A, B = slice(0, ka), slice(ka, ka + kb)

        def add(zz, _):
            L0[i][s, zz, y, :, A] = total(L0[i][s, zz, y, :, A], R2A[i][zz])
            if kb:
                L0[i][s, zz, y, :, B] = total(L0[i][s, zz, y, :, B], R2B[i][zz])
            return 0

        lax.fori_loop(0, Z, add, 0)
        state[i, 3] = [
            ship(
                L0[i].at[s, lax.rem(z + d, Z), y],
                outs[i].at[d],
                zs.at[i, d - 1],
                zr.at[i, d - 1],
                z_peers[d - 1],
            )
            for d in range(1, Z)
        ]

    def stage4(i):
        for copy in state[i, 3]:
            copy.wait_recv()
        outs[i][0] = L0[i][s, z, y]

    stages = (stage0, stage1, stage2, stage3, stage4)
    for t in range(n + 4):
        for k in range(5):
            if 0 <= t - k < n:
                stages[k](t - k)
    for copy in sends:
        copy.wait_send()


def scatter_all(arrays, Z):
    n = len(arrays)
    D = pltpu.SemaphoreType.DMA

    def buffers(shape_of):
        return [pltpu.VMEM(shape_of(*a.shape[4:]), BF16) for a in arrays]

    def half(columns, k):
        return max(halves(columns)[k], 128)

    return pl.pallas_call(
        functools.partial(scatter_kernel, n, Z),
        out_shape=[jax.ShapeDtypeStruct((Z,) + a.shape[4:], BF16) for a in arrays],
        in_specs=[pl.BlockSpec(memory_space=pl.ANY)] * n,
        out_specs=[pl.BlockSpec(memory_space=pltpu.VMEM)] * n,
        scratch_shapes=buffers(lambda r, k: (2, Z, 2, r, k))
        + buffers(lambda r, k: (2, Z, 2, r, k))
        + buffers(lambda r, k: (2, Z, r, half(k, 0)))
        + buffers(lambda r, k: (Z, 2, r, half(k, 1)))
        + buffers(lambda r, k: (Z, r, half(k, 0)))
        + buffers(lambda r, k: (Z, r, half(k, 1)))
        + [D((n,)), D((n,)), D((n,)), D((n, 4)), D((n, 4)), D((n, Z - 1)), D((n, Z - 1))],
        compiler_params=pltpu.CompilerParams(
            collective_id=1, has_side_effects=True, vmem_limit_bytes=60 * 2**20
        ),
    )(*arrays)


def nn(a, b): return jnp.dot(a, b, preferred_element_type=F32)
def nt(a, b): return lax.dot_general(a, b, (((1,), (1,)), ((), ())), preferred_element_type=F32)
def tn(a, b): return lax.dot_general(a, b, (((0,), (0,)), ((), ())), preferred_element_type=F32)

def norm_parts(x):
    center = x - jnp.mean(x, axis=-1, keepdims=True)
    r = lax.rsqrt(jnp.mean(center * center, axis=-1, keepdims=True) + NORM_EPS)
    return center * r, r

def norm_back(g, hat, r, gain):
    w = g * (1.0 + gain)
    return r * (w - jnp.mean(w, axis=-1, keepdims=True) - hat * jnp.mean(w * hat, axis=-1, keepdims=True))

def gelu_parts(z):
    x = jnp.abs(z) * math.sqrt(0.5)
    t = 1.0 / (1.0 + 0.3275911 * x)
    e = jnp.exp(-(x * x))
    poly = t * (0.254829592 + t * (-0.284496736 + t * (1.421413741 + t * (-1.453152027 + t * 1.061405429))))
    half = 0.5 * poly * e
    cdf = jnp.where(z > 0, 1.0 - half, half)
    return z * cdf, cdf + z * e * (1.0 / math.sqrt(2.0 * math.pi))

def col_sum(m): return jnp.sum(m, axis=0, keepdims=True)

def pick_matrix(places_row, keep_count, slots):
    pos = lax.broadcasted_iota(jnp.int32, (slots, ROWS_E), 0)
    r = lax.broadcasted_iota(jnp.int32, (slots, ROWS_E), 1)
    return ((pos == places_row) & (r < keep_count)).astype(BF16)

def enc_fwd_kernel(info, places, patches, gains, bias, qkv_h, proj_h, fc1_h, fc2_h,
                   enc_o, x_o, m_o, o_o, x1_o, u_o, dg_o, p_o, qkv, proj, fc1, fc2, sem):
    copies = [pltpu.make_async_copy(h, v, sem.at[i]) for i, (h, v) in enumerate(((qkv_h, qkv), (proj_h, proj), (fc1_h, fc1), (fc2_h, fc2)))]
    for cp in copies: cp.start()
    v = info[0] // 10
    pick = pick_matrix(places[...], v, patches.shape[0])
    x = tn(pick, patches[...])
    x_o[...] = x
    hat, _ = norm_parts(x)
    h = (hat * (1.0 + gains[0:1]) + gains[1:2]).astype(BF16)
    copies[0].wait()
    W = x.shape[1]
    m = nn(h, qkv[...])
    q = (m[:, :W] + gains[4:5]).astype(BF16)
    k = m[:, W:2*W].astype(BF16)
    val = (m[:, 2*W:] + gains[5:6]).astype(BF16)
    m_o[...] = jnp.concatenate([q, k, val], 1)
    live = lax.broadcasted_iota(jnp.int32, (ROWS_E, ROWS_E), 1) < v
    hs = W // HEADS_E
    outs = []
    for j in range(HEADS_E):
        sl = slice(hs*j, hs*(j+1))
        s = jnp.where(live, nt(q[:, sl], k[:, sl]) * hs**-0.5, FAR_BELOW)
        e = jnp.exp(s - jnp.max(s, axis=-1, keepdims=True))
        p = e / jnp.sum(e, axis=-1, keepdims=True)
        p_o[j] = p
        outs.append(nn(p.astype(BF16), val[:, sl]).astype(BF16))
    o = jnp.concatenate(outs, 1)
    o_o[...] = o
    copies[1].wait()
    x1 = x + (nn(o, proj[...]) + gains[6:7])
    x1_o[...] = x1
    hat2, _ = norm_parts(x1)
    h2 = (hat2 * (1.0 + gains[2:3]) + gains[3:4]).astype(BF16)
    copies[2].wait()
    u, dg = gelu_parts(nn(h2, fc1[...]) + bias[...])
    u = u.astype(BF16)
    u_o[...] = u; dg_o[...] = dg
    copies[3].wait()
    enc_o[...] = (x1 + (nn(u, fc2[...]) + gains[7:8])).astype(BF16)

V = pl.BlockSpec(memory_space=pltpu.VMEM); A = pl.BlockSpec(memory_space=pl.ANY); S = pl.BlockSpec(memory_space=pltpu.SMEM)
D = pltpu.SemaphoreType.DMA
def params(mb=56): return pltpu.CompilerParams(vmem_limit_bytes=mb*2**20)

def enc_fwd(info, places, patches, gains, bias, qkv, proj, fc1, fc2):
    W, Fw = fc1.shape
    sd = jax.ShapeDtypeStruct
    return pl.pallas_call(enc_fwd_kernel,
        out_shape=(sd((ROWS_E, W), BF16), sd((ROWS_E, W), F32), sd((ROWS_E, 3*W), BF16), sd((ROWS_E, W), BF16), sd((ROWS_E, W), F32),
                   sd((ROWS_E, Fw), BF16), sd((ROWS_E, Fw), F32), sd((HEADS_E, ROWS_E, ROWS_E), F32)),
        in_specs=[S, V, V, V, V, A, A, A, A], out_specs=(V,)*8,
        scratch_shapes=[pltpu.VMEM(w.shape, BF16) for w in (qkv, proj, fc1, fc2)] + [D((4,))],
        compiler_params=params())(info, places, patches, gains, bias, qkv, proj, fc1, fc2)

def enc_bwd_kernel(info, places, encoded, gemb, embed, gains, x_r, m_r, o_r, x1_r, u_r, dg_r, p_r, qkv_h, proj_h, fc1_h, fc2_h,
                   gp_o, gembed_o, gqkv_o, gproj_o, gfc1_o, gfc2_o, gvec_o, gbias_o,
                   qkv, proj, fc1, fc2, sfc2, sfc1, sproj, sqkv, sem):
    copies = [pltpu.make_async_copy(h, v, sem.at[i]) for i, (h, v) in enumerate(((fc2_h, fc2), (fc1_h, fc1), (proj_h, proj), (qkv_h, qkv)))]
    for cp in copies: cp.start()
    ge = gemb[...]
    gembed_o[...] = tn(encoded[...], ge).astype(BF16)
    gy = nt(ge, embed[...]).astype(BF16)
    G = gy.astype(F32)
    u = u_r[...]
    sfc2[...] = tn(u, gy).astype(BF16)
    w2 = pltpu.make_async_copy(sfc2, gfc2_o, sem.at[4]); w2.start()
    copies[0].wait()
    gz = (nt(gy, fc2[...]) * dg_r[...]).astype(BF16)
    gbias_o[...] = col_sum(gz.astype(F32))
    x1 = x1_r[...]
    hat2, r2 = norm_parts(x1)
    h2 = (hat2 * (1.0 + gains[2:3]) + gains[3:4]).astype(BF16)
    sfc1[...] = tn(h2, gz).astype(BF16)
    w1 = pltpu.make_async_copy(sfc1, gfc1_o, sem.at[5]); w1.start()
    copies[1].wait()
    gh2 = nt(gz, fc1[...])
    gvec_o[2:3, :] = col_sum(gh2 * hat2)
    gvec_o[3:4, :] = col_sum(gh2)
    gx1 = G + norm_back(gh2, hat2, r2, gains[2:3])
    ga = gx1.astype(BF16)
    gvec_o[6:7, :] = col_sum(ga.astype(F32))
    gvec_o[7:8, :] = col_sum(G)
    o = o_r[...]
    sproj[...] = tn(o, ga).astype(BF16)
    wp = pltpu.make_async_copy(sproj, gproj_o, sem.at[6]); wp.start()
    copies[2].wait()
    go = nt(ga, proj[...]).astype(BF16)
    W = x1.shape[1]
    hs = W // HEADS_E
    gq, gk, gv = [], [], []
    for j in range(HEADS_E):
        q = m_r[:, hs*j:hs*(j+1)]; k = m_r[:, W+hs*j:W+hs*(j+1)]; val = m_r[:, 2*W+hs*j:2*W+hs*(j+1)]
        g = go[:, hs*j:hs*(j+1)]
        p = p_r[j]
        gv.append(tn(p.astype(BF16), g).astype(BF16))
        gp = nt(g, val)
        gs = (p * (gp - jnp.sum(gp * p, axis=-1, keepdims=True))).astype(BF16)
        gq.append((nn(gs, k) * hs**-0.5).astype(BF16))
        gk.append((tn(gs, q) * hs**-0.5).astype(BF16))
    gm = jnp.concatenate(gq + gk + gv, 1)
    gvec_o[4:5, :] = col_sum(gm[:, :W].astype(F32))
    gvec_o[5:6, :] = col_sum(gm[:, 2*W:].astype(F32))
    x = x_r[...]
    hat, r = norm_parts(x)
    h = (hat * (1.0 + gains[0:1]) + gains[1:2]).astype(BF16)
    sqkv[...] = tn(h, gm).astype(BF16)
    wq = pltpu.make_async_copy(sqkv, gqkv_o, sem.at[7]); wq.start()
    copies[3].wait()
    gh = nt(gm, qkv[...])
    gvec_o[0:1, :] = col_sum(gh * hat)
    gvec_o[1:2, :] = col_sum(gh)
    gx = gx1 + norm_back(gh, hat, r, gains[0:1])
    pick = pick_matrix(places[...], info[0] // 10, gp_o.shape[0]).astype(F32)
    gp_o[...] = jnp.dot(pick, gx, preferred_element_type=F32, precision=lax.Precision.HIGHEST)
    for cp in (w2, w1, wp, wq): cp.wait()

def enc_bwd(info, places, encoded, gemb, embed, gains, x, m, o, x1, u, dg, p, qkv, proj, fc1, fc2, slots):
    W, Fw = fc1.shape
    sd = jax.ShapeDtypeStruct
    return pl.pallas_call(enc_bwd_kernel,
        out_shape=(sd((slots, W), F32), sd(embed.shape, BF16), sd(qkv.shape, BF16), sd(proj.shape, BF16), sd(fc1.shape, BF16), sd(fc2.shape, BF16), sd((8, W), F32), sd((1, Fw), F32)),
        in_specs=[S] + [V]*12 + [A]*4, out_specs=(V, V, A, A, A, A, V, V),
        scratch_shapes=[pltpu.VMEM(w.shape, BF16) for w in (qkv, proj, fc1, fc2, fc2, fc1, proj, qkv)] + [D((8,))],
        compiler_params=params())(info, places, encoded, gemb, embed, gains, x, m, o, x1, u, dg, p, qkv, proj, fc1, fc2)

def dec_pre_kernel(info, places, encoded, embed, gains, posT, qkv, x_o, q_o, k_o, v_o):
    n = x_o.shape[0]
    i = pl.program_id(0)
    emb = nn(encoded[...], embed[...]) + gains[8:9]
    pos_i = lax.broadcasted_iota(jnp.int32, (n, ROWS_E), 0) + i * n
    r = lax.broadcasted_iota(jnp.int32, (n, ROWS_E), 1)
    pick = ((pos_i == places[...]) & (r < info[0] // 10)).astype(F32)
    seen = jnp.sum(pick, axis=1, keepdims=True)
    placed = jnp.dot(pick, emb, preferred_element_type=F32, precision=lax.Precision.HIGHEST)
    x = placed + (1.0 - seen) * gains[9:10] + posT[...].T.astype(F32)
    x_o[...] = x
    hat, _ = norm_parts(x)
    h = (hat * (1.0 + gains[0:1]) + gains[1:2]).astype(BF16)
    m = nn(h, qkv[...])
    W = x.shape[1]
    q_o[...] = (m[:, :W] + gains[4:5]).astype(BF16)
    k_o[...] = (m[:, W:2*W] * (HD**-0.5 * math.log2(math.e))).astype(BF16)
    v_o[...] = (m[:, 2*W:] + gains[5:6]).astype(BF16)

def dec_pre(info, places, encoded, embed, gains, posT, qkv, tile=512):
    W, n = posT.shape
    sd = jax.ShapeDtypeStruct
    full = lambda a: pl.BlockSpec(a.shape, lambda i: (0,)*a.ndim)
    row = pl.BlockSpec((tile, W), lambda i: (i, 0))
    return pl.pallas_call(dec_pre_kernel, grid=(n//tile,),
        out_shape=(sd((n, W), F32),) + (sd((n, W), BF16),)*3,
        in_specs=[S, full(places), full(encoded), full(embed), full(gains), pl.BlockSpec((W, tile), lambda i: (0, i)), full(qkv)],
        out_specs=(row,)*4, compiler_params=params())(info, places, encoded, embed, gains, posT, qkv)

def head_rows(block, j):
    parts = []
    if j > 0: parts.append(jnp.zeros((HD*j, block.shape[1]), block.dtype))
    parts.append(block[HD*j:HD*(j+1)])
    if j < 3: parts.append(jnp.zeros((HD*(3-j), block.shape[1]), block.dtype))
    return jnp.concatenate(parts, 0)

def head_lanes(block, j):
    lane = lax.broadcasted_iota(jnp.int32, block.shape, 1)
    return jnp.where((lane >= HD*j) & (lane < HD*(j+1)), block, jnp.zeros_like(block))

def dead_bias(count, n):
    return jnp.where(lax.broadcasted_iota(jnp.int32, (n - SHORT, 1), 0) + SHORT < count, 0.0, FAR_BELOW)

def attend_kernel(info, q_ref, k_ref, v_ref, o_ref, L_ref):
    k = k_ref[...]
    bias = dead_bias(info[0], k.shape[0])
    qT = q_ref[...].T
    vT = v_ref[...].T
    outs = []
    for j in range(4):
        rows = slice(HD*j, HD*(j+1))
        s = nn(k, head_rows(qT, j))
        s = jnp.concatenate([s[:SHORT], s[SHORT:] + bias], 0)
        m = jnp.max(s, axis=0, keepdims=True)
        p = jnp.exp2(s - m)
        total = jnp.sum(p, axis=0, keepdims=True)
        o = nn(vT[rows], p.astype(BF16))
        outs.append((o * (1.0 / total)).astype(BF16))
        L_ref[0, j:j+1, :] = m + jnp.log2(total)
    o_ref[...] = jnp.concatenate(outs, 0).T

def attend(info, q, k, v):
    n, W = k.shape
    blk = pl.BlockSpec((n, GROUP), lambda g: (0, g))
    return pl.pallas_call(attend_kernel, grid=(W//GROUP,),
        out_shape=(jax.ShapeDtypeStruct((n, W), BF16), jax.ShapeDtypeStruct((W//GROUP, 4, n), F32)),
        in_specs=[S, blk, blk, blk], out_specs=(blk, pl.BlockSpec((1, 4, n), lambda g: (g, 0, 0))),
        compiler_params=params())(info, q, k, v)

def attend_back_kernel(info, q_ref, k_ref, v_ref, go_ref, o_ref, L_ref, gq_ref, gk_ref, gv_ref):
    q = q_ref[...]; k = k_ref[...]; v = v_ref[...]; go = go_ref[...]
    bias = dead_bias(info[0], k.shape[0])
    qT = q.T; kT = k.T; goT = go.T; oT = o_ref[...].T
    inner_all = goT.astype(F32) * oT.astype(F32)
    ak = av = None
    gqs = []
    for j in range(4):
        rows = slice(HD*j, HD*(j+1))
        s = nn(k, head_rows(qT, j))
        s = jnp.concatenate([s[:SHORT], s[SHORT:] + bias], 0)
        p = jnp.exp2(s - L_ref[0, j:j+1, :])
        gp = nn(v, head_rows(goT, j))
        inner = jnp.sum(inner_all[rows], axis=0, keepdims=True)
        gs = (p * (gp - inner)).astype(BF16)
        a = nn(p.astype(BF16), head_lanes(go, j))
        b = nn(gs, head_lanes(q, j))
        av = a if av is None else av + a
        ak = b if ak is None else ak + b
        gqs.append((nn(kT[rows], gs) * math.log(2.0)).astype(BF16))
    gq_ref[...] = jnp.concatenate(gqs, 0).T
    gk_ref[...] = (ak * HD**-0.5).astype(BF16)
    gv_ref[...] = av.astype(BF16)

def attend_back(info, q, k, v, go, o, L):
    n, W = k.shape
    blk = pl.BlockSpec((n, GROUP), lambda g: (0, g))
    return pl.pallas_call(attend_back_kernel, grid=(W//GROUP,),
        out_shape=(jax.ShapeDtypeStruct((n, W), BF16),)*3,
        in_specs=[S, blk, blk, blk, blk, blk, pl.BlockSpec((1, 4, n), lambda g: (g, 0, 0))], out_specs=(blk,)*3,
        compiler_params=params())(info, q, k, v, go, o, L)

def dec_mid_kernel(steps, info, x_r, o_r, cot_r, gains, bias, proj, fc1, fc2,
                   dec_o, gx1_o, go_o, gfc2_o, gfc1_o, gproj_o, gvec_o, gbias_o, afc2, afc1, aproj):
    i = pl.program_id(0)
    @pl.when(i == 0)
    def _():
        for ref in (afc2, afc1, aproj, gvec_o, gbias_o): ref[...] = jnp.zeros_like(ref)
    n = x_r.shape[0]
    live = lax.broadcasted_iota(jnp.int32, (n, 1), 0) + i * n < info[0]
    o = o_r[...]
    x1 = x_r[...] + (nn(o, proj[...]) + gains[6:7])
    hat, r = norm_parts(x1)
    h2 = (hat * (1.0 + gains[2:3]) + gains[3:4]).astype(BF16)
    u, dg = gelu_parts(nn(h2, fc1[...]) + bias[...])
    u = u.astype(BF16)
    y = x1 + (nn(u, fc2[...]) + gains[7:8])
    dec_o[...] = jnp.where(live, y, 0.0).astype(BF16)
    G = jnp.where(live, cot_r[...].astype(F32), 0.0)
    gy = G.astype(BF16)
    afc2[...] += tn(u, gy)
    gz = (nt(gy, fc2[...]) * dg).astype(BF16)
    gbias_o[...] += col_sum(gz.astype(F32))
    afc1[...] += tn(h2, gz)
    gh2 = nt(gz, fc1[...])
    gvec_o[0:1, :] += col_sum(gh2 * hat)
    gvec_o[1:2, :] += col_sum(gh2)
    gx1 = G + norm_back(gh2, hat, r, gains[2:3])
    gx1_o[...] = gx1
    ga = gx1.astype(BF16)
    gvec_o[2:3, :] += col_sum(ga.astype(F32))
    gvec_o[3:4, :] += col_sum(G)
    aproj[...] += tn(o, ga)
    go_o[...] = nt(ga, proj[...]).astype(BF16)
    @pl.when(i == steps - 1)
    def _():
        gfc2_o[...] = afc2[...].astype(BF16)
        gfc1_o[...] = afc1[...].astype(BF16)
        gproj_o[...] = aproj[...].astype(BF16)

def dec_mid(info, x, o, cot, gains, bias, proj, fc1, fc2, tile=256):
    n, W = x.shape
    sd = jax.ShapeDtypeStruct
    full = lambda a: pl.BlockSpec(a.shape, lambda i: (0,)*a.ndim)
    row = pl.BlockSpec((tile, W), lambda i: (i, 0))
    Fw = fc1.shape[1]
    outs = (sd((n, W), BF16), sd((n, W), F32), sd((n, W), BF16), sd(fc2.shape, BF16), sd(fc1.shape, BF16), sd(proj.shape, BF16), sd((8, W), F32), sd((1, Fw), F32))
    return pl.pallas_call(functools.partial(dec_mid_kernel, n//tile), grid=(n//tile,), out_shape=outs,
        in_specs=[S, row, row, row, full(gains), full(bias), full(proj), full(fc1), full(fc2)],
        out_specs=(row, row, row) + tuple(full(a) for a in outs[3:]),
        scratch_shapes=[pltpu.VMEM(w.shape, F32) for w in (fc2, fc1, proj)],
        compiler_params=params())(info, x, o, cot, gains, bias, proj, fc1, fc2)

def dec_post_kernel(steps, info, places, x_r, gx1_r, gq_r, gk_r, gv_r, gains, qkv, gqkv_o, gposT_o, gemb_o, gvec_o, aqkv, aemb):
    i = pl.program_id(0)
    @pl.when(i == 0)
    def _():
        for ref in (aqkv, aemb, gvec_o): ref[...] = jnp.zeros_like(ref)
    n = x_r.shape[0]
    x = x_r[...]
    hat, r = norm_parts(x)
    h = (hat * (1.0 + gains[0:1]) + gains[1:2]).astype(BF16)
    gm = jnp.concatenate([gq_r[...], gk_r[...], gv_r[...]], 1)
    W = x.shape[1]
    aqkv[...] += tn(h, gm)
    gh = nt(gm, qkv[...])
    gvec_o[0:1, :] += col_sum(gh * hat)
    gvec_o[1:2, :] += col_sum(gh)
    gvec_o[4:5, :] += col_sum(gq_r[...].astype(F32))
    gvec_o[5:6, :] += col_sum(gv_r[...].astype(F32))
    gx = gx1_r[...] + norm_back(gh, hat, r, gains[0:1])
    gxb = gx.astype(BF16)
    gposT_o[...] = gxb.T
    pos_i = lax.broadcasted_iota(jnp.int32, (n, ROWS_E), 0) + i * n
    rr = lax.broadcasted_iota(jnp.int32, (n, ROWS_E), 1)
    pick = ((pos_i == places[...]) & (rr < info[0] // 10)).astype(BF16)
    seen = jnp.sum(pick.astype(F32), axis=1, keepdims=True)
    aemb[...] += tn(pick, gxb)
    gvec_o[9:10, :] += col_sum(gx * (1.0 - seen))
    @pl.when(i == steps - 1)
    def _():
        gqkv_o[...] = aqkv[...].astype(BF16)
        gemb_o[...] = aemb[...].astype(BF16)
        gvec_o[8:9, :] = col_sum(aemb[...])

def dec_post(info, places, x, gx1, gq, gk, gv, gains, qkv, tile=256):
    n, W = x.shape
    sd = jax.ShapeDtypeStruct
    full = lambda a: pl.BlockSpec(a.shape, lambda i: (0,)*a.ndim)
    row = pl.BlockSpec((tile, W), lambda i: (i, 0))
    outs = (sd(qkv.shape, BF16), sd((W, n), BF16), sd((ROWS_E, W), BF16), sd((16, W), F32))
    return pl.pallas_call(functools.partial(dec_post_kernel, n//tile), grid=(n//tile,), out_shape=outs,
        in_specs=[S, full(places), row, row, row, row, row, full(gains), full(qkv)],
        out_specs=(full(outs[0]), pl.BlockSpec((W, tile), lambda i: (0, i)), full(outs[2]), full(outs[3])),
        scratch_shapes=[pltpu.VMEM(qkv.shape, F32), pltpu.VMEM((ROWS_E, W), F32)],
        compiler_params=params())(info, places, x, gx1, gq, gk, gv, gains, qkv)


def unpack_kernel(small, e_gains, e_bias, d_gains, d_bias):
    count = small.shape[0]
    values = small[...].astype(F32)
    for out, row, rows in ((e_gains, 0, 8), (d_gains, 8, 16), (e_bias, 24, 1), (d_bias, 25, 1)):
        w = out.shape[1] // count
        out[...] = jnp.concatenate([values[i, row : row + rows, :w] for i in range(count)], 1)


def unpack(small, shapes):
    return pl.pallas_call(
        unpack_kernel, out_shape=[jax.ShapeDtypeStruct(s, F32) for s in shapes]
    )(small)


def pack_kernel(e_vec, e_bias, mid_vec, post_vec, d_bias, out, whole):
    count = out.shape[0]
    whole[...] = jnp.zeros_like(whole)
    whole[0:2] = post_vec[0:2]
    whole[2:4] = mid_vec[0:2]
    whole[4:6] = post_vec[4:6]
    whole[6:8] = mid_vec[2:4]
    whole[8:10] = post_vec[8:10]
    out[...] = jnp.zeros_like(out)
    for ref, row, rows in ((e_vec, 0, 8), (whole, 8, 16), (e_bias, 24, 1), (d_bias, 25, 1)):
        w = ref.shape[1] // count
        values = ref[...].astype(BF16)
        for i in range(count):
            out[i, row : row + rows, :w] = values[:, w * i : w * i + w]


def pack(e_vec, e_bias, mid_vec, post_vec, d_bias, count):
    return pl.pallas_call(
        pack_kernel,
        out_shape=jax.ShapeDtypeStruct((count, SMALL_ROWS, 128), BF16),
        scratch_shapes=[pltpu.VMEM((16, mid_vec.shape[1]), F32)],
    )(e_vec, e_bias, mid_vec, post_vec, d_bias)


def last_kernel(n, *refs):
    ins, outs = refs[:n], refs[n:]

    def total(ref):
        acc = ref[0].astype(F32)
        for d in range(1, ref.shape[0]):
            acc = acc + ref[d].astype(F32)
        return acc

    small = total(ins[0])
    for out, row in zip(outs[:4], (0, 8, 24, 25)):
        out[...] = small[row : row + out.shape[0], : out.shape[1]]
    for i, ref in enumerate(ins[1:]):
        outs[4 + i][...] = total(ref).T if i == POS_AT else total(ref)


def last_sums(arrays, shapes):
    return pl.pallas_call(
        functools.partial(last_kernel, len(arrays)),
        out_shape=[jax.ShapeDtypeStruct(s, F32) for s in shapes],
        compiler_params=params(),
    )(*arrays)


def body(
    patches,
    lengths,
    keep_order,
    e_vectors,
    e_qkv,
    e_proj,
    e_fc1,
    e_fc1_bias,
    e_fc2,
    embed,
    d_vectors,
    dec_pos,
    d_qkv,
    d_proj,
    d_fc1,
    d_fc1_bias,
    d_fc2,
    cotangent,
):
    count = lax.axis_size("segment") * lax.axis_size("dp")
    Z = lax.axis_size("dp") // 4
    cube = lax.axis_index(AXES)
    slots = patches.shape[1]
    smalls = (e_vectors, d_vectors, e_fc1_bias.reshape(1, -1), d_fc1_bias.reshape(1, -1))
    shards = (e_qkv, e_proj, e_fc1, e_fc2, embed, dec_pos, d_qkv, d_proj, d_fc1, d_fc2)
    full = gather_all(smalls, shards, Z)
    e_gains, e_bias, d_gains, d_bias = unpack(
        full[0].reshape(count, SMALL_ROWS, 128),
        [
            (8, e_vectors.shape[1] * count),
            (1, e_fc1_bias.shape[0] * count),
            (16, d_vectors.shape[1] * count),
            (1, d_fc1_bias.shape[0] * count),
        ],
    )
    mats = [m.reshape(-1, m.shape[-1]) for m in full[1:]]
    w_qkv, w_proj, w_fc1, w_fc2, w_embed, posT, dw_qkv, dw_proj, dw_fc1, dw_fc2 = mats

    info = lax.dynamic_slice_in_dim(lengths, cube, 1, 0)
    places = lax.dynamic_slice_in_dim(keep_order, cube, 1, 0)[:, :ROWS_E]
    encoded, *kept = enc_fwd(
        info, places, patches[0], e_gains, e_bias, w_qkv, w_proj, w_fc1, w_fc2
    )
    x, q, k, v = dec_pre(info, places, encoded, w_embed, d_gains, posT, dw_qkv)
    o, L = attend(info, q, k, v)
    decoded, gx1, go, gd_fc2, gd_fc1, gd_proj, mid_vec, gd_bias = dec_mid(
        info, x, o, cotangent[0], d_gains, d_bias, dw_proj, dw_fc1, dw_fc2
    )
    gq, gk, gv = attend_back(info, q, k, v, go, o, L)
    gd_qkv, g_posT, gemb, post_vec = dec_post(
        info, places, x, gx1, gq, gk, gv, d_gains, dw_qkv
    )
    g_patch, g_embed, ge_qkv, ge_proj, ge_fc1, ge_fc2, e_vec, ge_bias = enc_bwd(
        info, places, encoded, gemb, w_embed, e_gains, *kept, w_qkv, w_proj, w_fc1, w_fc2, slots
    )
    g_small = pack(e_vec, ge_bias, mid_vec, post_vec, gd_bias, count)

    def blocks(m):
        return m.reshape((2, Z, 2, 2, -1, m.shape[-1]))

    order = (gd_fc2, gd_fc1, gd_proj, gd_qkv, g_posT, g_embed, ge_fc2, ge_fc1, ge_proj, ge_qkv)
    parts = scatter_all([blocks(m) for m in order + (g_small.reshape(-1, 128),)], Z)
    shapes = [m.shape for m in smalls + shards]
    out = last_sums(parts[::-1], shapes)
    re_vec, rd_vec, re_bias, rd_bias = out[:4]
    re_qkv, re_proj, re_fc1, re_fc2, r_embed, r_pos, rd_qkv, rd_proj, rd_fc1, rd_fc2 = out[4:]
    return (
        decoded[None],
        g_patch[None],
        re_vec,
        re_qkv,
        re_proj,
        re_fc1,
        re_bias.reshape(-1),
        re_fc2,
        r_embed,
        rd_vec,
        r_pos,
        rd_qkv,
        rd_proj,
        rd_fc1,
        rd_bias.reshape(-1),
        rd_fc2,
    )


def solution(mesh):
    rows, columns, cubes = P(AXES, None), P(None, AXES), P(AXES, None, None)
    weights = (columns, rows, rows, rows, P(AXES), rows, rows, columns, columns)
    weights = weights + (rows, rows, rows, P(AXES), rows)
    return jax.shard_map(
        body,
        mesh=mesh,
        in_specs=(cubes, P(), P()) + weights + (cubes,),
        out_specs=(cubes, cubes) + weights,
        check_vma=False,
    )
```

time: 526 us -> 417 us (0.79)
  matrix products: 106 us -> 0 us
  Pallas kernels: 302 us -> 404 us
  local copies, waits for them, and re-layouts: 61.3 us -> 5.48 us
  other arithmetic: 42.6 us -> 0 us
    dot_general x32 -> x0, matrix products: 105 us -> none  [mm(): return jnp.einsum(spec, a, b, preferred_element_type=F32)]
    pallas_call x2 -> x10, Pallas kernels: 65.8 us -> 167 us  [the longest x1 44.9 us: attend_back(): pl.pallas_call(attend_back_kernel, grid=(W // GROUP,), out_shape=(jax.Sha...]
    unnamed x186 -> x6, local copies, waits for them, and re-layouts: 31.4 us -> 3.69 us
    convert_element_type x16 -> x0, other arithmetic: 20.7 us -> none  [the longest x11 15.9 us: body(): full = gather_all([m.astype(BF16) for m in sent], Z)]
    reduce_sum x17 -> x0, other arithmetic: 11.4 us -> none  [the longest x5 4.61 us: norm_rows(): center = values - jnp.mean(values, axis=-1, keepdims=True)]
where the time goes in v2:
time: 417 us; the launch traced here: 410 us
  Pallas kernels  404 us (97%)
  local copies, waits for them, and re-layouts  5.48 us (1%)
    pallas_call x1, Pallas kernels, scatter_all(): pl.pallas_call(functools.partial(scatter_kernel, n, Z), out_shape=[jax.Sh...  119 us
    pallas_call x1, Pallas kernels, gather_all(): pl.pallas_call(functools.partial(gather_kernel, n, Z), out_shape=[jax.Sha...  118 us
    pallas_call x1, Pallas kernels, attend_back(): pl.pallas_call(attend_back_kernel, grid=(W // GROUP,), out_shape=(jax.Sha...  44.9 us
    pallas_call x1, Pallas kernels, dec_mid(): pl.pallas_call(functools.partial(dec_mid_kernel, n // tile), grid=(n // t...  31.8 us
    pallas_call x1, Pallas kernels, attend(): pl.pallas_call(attend_kernel, grid=(W // GROUP,), out_shape=(jax.ShapeDty...  26 us
    pallas_call x1, Pallas kernels, enc_bwd(): pl.pallas_call(enc_bwd_kernel, out_shape=(sd((slots, W), F32), sd(embed.s...  24.2 us
    pallas_call x1, Pallas kernels, enc_fwd(): pl.pallas_call(enc_fwd_kernel, out_shape=(sd((ROWS_E, W), BF16), sd((ROWS...  13.4 us
    pallas_call x1, Pallas kernels, dec_post(): pl.pallas_call(functools.partial(dec_post_kernel, n // tile), grid=(n //...  11.6 us

profile of v2, /device:TPU:0, one launch (start us, length us, event | category | flops | bytes accessed | tf_op | source)
XLA Modules:
  0.0 410.0 jit_solution(12477920768442356021)
XLA Ops:
  0.6 0.0 copy-start
  0.7 1.3 dynamic_slice.6.info
  1.9 0.0 copy-done
  1.9 0.5 constant_dynamic-slice_fusion.places
  2.5 1.8 copy.34.refs_9_
  4.3 117.9 %shard_map.297 = (bf16[2,4,2,2,32,128]{5,4,3,2,1,0:T(8,128)(2,1)}, bf16[2,4,2,2,24,2304]{5,4,3,2,1,0:T(8,128)(2,1)}, bf16[2,4,2,2,24,768]{5,4,3,2,1,0:T(8,128)(2...) custom-call(f32[8,24]{1,0:T(8,128)} %refs_0_.1, ...), custom_call_target="tpu_custom_call" | custom-call | tf_op jit(solution)/shard_map/pallas_call | solution.py:160
  122.2 1.7 shard_map.298
  123.9 13.4 %shard_map.299 = (bf16[128,768]{1,0:T(8,128)(2,1)}, f32[128,768]{1,0:T(8,128)}, bf16[128,2304]{1,0:T(8,128)(2,1)}, bf16[128,768]{1,0:T(8,128)(2,1)}, f32[128,768...) custom-call(s32[1]{0:T(128)} %dynamic_slice.6.info, ...), custom_call_target="tpu_custom_call" | custom-call | tf_op jit(solution)/shard_map/pallas_call | solution.py:390
  137.3 8.7 %shard_map.300 = (f32[1024,512]{1,0:T(8,128)}, bf16[1024,512]{1,0:T(8,128)(2,1)}, bf16[1024,512]{1,0:T(8,128)(2,1)}, bf16[1024,512]{1,0:T(8,128)(2,1)}) custom-call(s32[1]{0:T(128)} %dynamic_slice.6.info, s32[1,128]{1,0:T(1,128)} %constant_dynamic-slice_fusion.places, bf16[128,768]{1,0:T(8,128)(2,1)} %get-tuple-element.100.encoded, ...), custom_call_target="tpu_custom_call" | custom-call | tf_op jit(solution)/shard_map/pallas_call | solution.py:492
  146.0 26.0 %shard_map.301 = (bf16[1024,512]{1,0:T(8,128)(2,1)}, f32[4,4,1024]{2,1,0:T(4,128)}) custom-call(s32[1]{0:T(128)} %dynamic_slice.6.info, bf16[1024,512]{1,0:T(8,128)(2,1)} %get-tuple-element.106.q_ref, bf16[1024,512]{1,0:T(8,128)(2,1)} %get-tuple-element.107.k_ref, bf16[1024,512]{1,0:T(8,128)(2,1)} %get-tuple-element.108.v_ref), custom_call_target="tpu_custom_call" | custom-call | tf_op jit(solution)/shard_map/pallas_call | solution.py:532
  171.9 31.8 %shard_map.302 = (bf16[1024,512]{1,0:T(8,128)(2,1)}, f32[1024,512]{1,0:T(8,128)}, bf16[1024,512]{1,0:T(8,128)(2,1)}, bf16[2048,512]{1,0:T(8,128)(2,1)}, bf16[512...) custom-call(s32[1]{0:T(128)} %dynamic_slice.6.info, ...), custom_call_target="tpu_custom_call" | custom-call | tf_op jit(solution)/shard_map/pallas_call | solution.py:614
  203.7 44.9 %shard_map.303 = (bf16[1024,512]{1,0:T(8,128)(2,1)}, bf16[1024,512]{1,0:T(8,128)(2,1)}, bf16[1024,512]{1,0:T(8,128)(2,1)}) custom-call(s32[1]{0:T(128)} %dynamic_slice.6.info, bf16[1024,512]{1,0:T(8,128)(2,1)} %get-tuple-element.106.q_ref, bf16[1024,512]{1,0:T(8,128)(2,1)} %get-tuple-element.107.k_ref, bf16[1024,512]{1,0:T(8,128)(2,1)} %get-tuple-element.108.v_ref, ...), custom_call_target="tpu_custom_call" | custom-call | tf_op jit(solution)/shard_map/pallas_call | solution.py:564
  248.6 11.6 %shard_map.304 = (bf16[512,1536]{1,0:T(8,128)(2,1)}, bf16[512,1024]{1,0:T(8,128)(2,1)}, bf16[128,512]{1,0:T(8,128)(2,1)}, f32[16,512]{1,0:T(8,128)}) custom-call(s32[1]{0:T(128)} %dynamic_slice.6.info, s32[1,128]{1,0:T(1,128)} %constant_dynamic-slice_fusion.places, f32[1024,512]{1,0:T(8,128)} %get-tuple-element.105.x_r, ...), custom_call_target="tpu_custom_call" | custom-call | tf_op jit(solution)/shard_map/pallas_call | solution.py:658
  260.3 24.2 %shard_map.305 = (f32[1024,768]{1,0:T(8,128)}, bf16[768,512]{1,0:T(8,128)(2,1)}, bf16[768,2304]{1,0:T(8,128)(2,1)}, bf16[768,768]{1,0:T(8,128)(2,1)}, bf16[768,3...) custom-call(s32[1]{0:T(128)} %dynamic_slice.6.info, ...), custom_call_target="tpu_custom_call" | custom-call | tf_op jit(solution)/shard_map/pallas_call | solution.py:462
  284.5 1.7 shard_map.306
  286.2 0.0 copy-start.1
  286.2 118.5 %shard_map.307 = (bf16[4,64,512]{2,1,0:T(8,128)(2,1)}, bf16[4,16,2048]{2,1,0:T(8,128)(2,1)}, bf16[4,16,512]{2,1,0:T(8,128)(2,1)}, bf16[4,16,1536]{2,1,0:T(8,128)...) custom-call(bf16[2,4,2,2,64,512]{5,4,3,2,1,0:T(8,128)(2,1)} %bitcast, ...), custom_call_target="tpu_custom_call" | custom-call | tf_op jit(solution)/shard_map/pallas_call | solution.py:295
  404.7 3.2 shard_map.308
  407.9 1.8 copy.35
  409.7 0.0 copy-done.1
Async XLA Ops:
  0.6 1.3 copy-start
  286.2 123.6 %copy-start.1 = (s32[32,1024]{1,0:T(8,128)S(1)}, s32[32,1024]{1,0:T(8,128)}, u32[]{:S(2)}) copy-start(s32[32,1024]{1,0:T(8,128)} %param.20) | copy-start | bytes 393220

commit v3 on v2

--- a/solution.py
+++ b/solution.py
@@ -180,134 +180,185 @@
     )(*small_shards, *arrays)
 
 
-def scatter_kernel(n, Z, *refs):
-    ins, outs = refs[:n], refs[n : 2 * n]
-    L0, R0, R1A, R1B, R2A, R2B = [refs[(2 + i) * n : (3 + i) * n] for i in range(6)]
-    loc, cs, cr, ms, mr, zs, zr = refs[8 * n :]
-    s, z, y, c = place()
-    X, Y, C = device(1 - s, z, y, c), device(s, z, 1 - y, c), device(s, z, y, 1 - c)
-    z_peers = [device(s, lax.rem(z + d, Z), y, c) for d in range(1, Z)]
-    greet(z_peers + [X, Y, C])
-    state = {}
-    sends = []
-
-    def ship(src, dst, ss, rs, target):
-        copy = send(src, dst, ss, rs, target)
-        sends.append(copy)
-        return copy
-
-    def total(a, b):
-        return (a.astype(F32) + b.astype(F32)).astype(BF16)
-
-    def stage0(i):
-        own = pltpu.make_async_copy(ins[i].at[:, :, :, c], L0[i], loc.at[i])
-        own.start()
-        state[i, 0] = (own, ship(ins[i].at[:, :, :, 1 - c], R0[i], cs.at[i], cr.at[i], C))
-
-    def stage1(i):
-        own, copy = state[i, 0]
-        own.wait()
-        copy.wait_recv()
-        ka, kb = halves(ins[i].shape[-1])
-
-        def add(t, _):
-            at = (t // (Z * 2), (t // 2) % Z, t % 2)
-            L0[i][at] = total(L0[i][at], R0[i][at])
-            return 0
-
-        lax.fori_loop(0, 4 * Z, add, 0)
-        A, B = pl.ds(0, ka), pl.ds(ka, kb)
-        state[i, 1] = [ship(L0[i].at[:, :, 1 - y, :, A], R1A[i], ms.at[i, 0], mr.at[i, 0], Y)]
-        if kb:
-            state[i, 1].append(
-                ship(L0[i].at[1 - s, :, :, :, B], R1B[i], ms.at[i, 1], mr.at[i, 1], X)
-            )
-
-    def stage2(i):
-        for copy in state[i, 1]:
-            copy.wait_recv()
-        ka, kb = halves(ins[i].shape[-1])
-        A, B = slice(0, ka), slice(ka, ka + kb)
-
-        def add(t, _):
-            u, zz = t // Z, t % Z
-            L0[i][u, zz, y, :, A] = total(L0[i][u, zz, y, :, A], R1A[i][u, zz])
+class Scatter:
+    def __init__(self, Z, arrays, chunks, sems):
+        self.Z, self.arrays, self.chunks = Z, arrays, chunks
+        self.loc, self.cs, self.cr, self.ms, self.mr, self.zs, self.zr = sems
+        self.s, self.z, self.y, self.c = s, z, y, c = place()
+        self.X, self.Y = device(1 - s, z, y, c), device(s, z, 1 - y, c)
+        self.C = device(s, z, y, 1 - c)
+        self.z_peers = [device(s, lax.rem(z + d, Z), y, c) for d in range(1, Z)]
+
+    def greet(self):
+        greet(self.z_peers + [self.X, self.Y, self.C])
+
+    def parts(self, m):
+        i, start, width = self.chunks[m]
+        ka, kb = halves(width)
+        return i, start, width, ka, kb, (start // 2 if kb else start)
+
+    def held(self, i, index, columns):
+        blocks, held = self.arrays[i][:2]
+        if held is None:
+            ss, zz, yy = index
+            return blocks.at[ss, zz, yy, self.c, :, columns]
+        return held.at[(*index, slice(None), columns)]
+
+    def copy(self, src, dst, ss, rs, target):
+        return pltpu.make_async_remote_copy(
+            src_ref=src,
+            dst_ref=dst,
+            send_sem=ss,
+            recv_sem=rs,
+            device_id=target,
+            device_id_type=MESH,
+        )
+
+    def own(self, m):
+        i, start, width, *_ = self.parts(m)
+        blocks, held = self.arrays[i][:2]
+        if held is None:
+            return None
+        cols = pl.ds(start, width)
+        return pltpu.make_async_copy(
+            blocks.at[:, :, :, self.c, :, cols], held.at[:, :, :, :, cols], self.loc.at[m]
+        )
+
+    def copies(self, m, stage):
+        i, start, width, ka, kb, at = self.parts(m)
+        s, z, y, c, Z = self.s, self.z, self.y, self.c, self.Z
+        blocks, held, R0, R1A, R1B, R2A, R2B, out = self.arrays[i]
+        cols, A, B = pl.ds(start, width), pl.ds(start, ka), pl.ds(start + ka, kb)
+        half = pl.ds(at, ka)
+        full = slice(None)
+        if stage == 0:
+            return [
+                self.copy(
+                    blocks.at[:, :, :, 1 - c, :, cols],
+                    R0.at[:, :, :, :, cols],
+                    self.cs.at[m],
+                    self.cr.at[m],
+                    self.C,
+                )
+            ]
+        if stage == 1:
+            made = [(self.held(i, (full, full, 1 - y), A), R1A.at[:, :, :, half], self.Y)]
             if kb:
-                L0[i][s, zz, u, :, B] = total(L0[i][s, zz, u, :, B], R1B[i][zz, u])
-            return 0
-
-        lax.fori_loop(0, 2 * Z, add, 0)
-        A, B = pl.ds(0, ka), pl.ds(ka, kb)
-        state[i, 2] = [ship(L0[i].at[1 - s, :, y, :, A], R2A[i], ms.at[i, 2], mr.at[i, 2], X)]
-        if kb:
-            state[i, 2].append(
-                ship(L0[i].at[s, :, 1 - y, :, B], R2B[i], ms.at[i, 3], mr.at[i, 3], Y)
-            )
-
-    def stage3(i):
-        for copy in state[i, 2]:
-            copy.wait_recv()
-        ka, kb = halves(ins[i].shape[-1])
-        A, B = slice(0, ka), slice(ka, ka + kb)
-
-        def add(zz, _):
-            L0[i][s, zz, y, :, A] = total(L0[i][s, zz, y, :, A], R2A[i][zz])
+                made.append((self.held(i, (1 - s, full, full), B), R1B.at[:, :, :, half], self.X))
+        elif stage == 2:
+            made = [(self.held(i, (1 - s, full, y), A), R2A.at[:, :, half], self.X)]
             if kb:
-                L0[i][s, zz, y, :, B] = total(L0[i][s, zz, y, :, B], R2B[i][zz])
-            return 0
-
-        lax.fori_loop(0, Z, add, 0)
-        state[i, 3] = [
-            ship(
-                L0[i].at[s, lax.rem(z + d, Z), y],
-                outs[i].at[d],
-                zs.at[i, d - 1],
-                zr.at[i, d - 1],
-                z_peers[d - 1],
-            )
-            for d in range(1, Z)
+                made.append((self.held(i, (s, full, 1 - y), B), R2B.at[:, :, half], self.Y))
+        else:
+            return [
+                self.copy(
+                    self.held(i, (s, lax.rem(z + d, Z), y), cols),
+                    out.at[d, :, cols],
+                    self.zs.at[m, d - 1],
+                    self.zr.at[m, d - 1],
+                    self.z_peers[d - 1],
+                )
+                for d in range(1, Z)
+            ]
+        k = 2 * (stage - 1)
+        return [
+            self.copy(src, dst, self.ms.at[m, k + j], self.mr.at[m, k + j], target)
+            for j, (src, dst, target) in enumerate(made)
         ]
 
-    def stage4(i):
-        for copy in state[i, 3]:
-            copy.wait_recv()
-        outs[i][0] = L0[i][s, z, y]
-
-    stages = (stage0, stage1, stage2, stage3, stage4)
-    for t in range(n + 4):
+    def add(self, i, index, columns, other):
+        ref = self.held(i, index, columns)
+        ref[...] = (ref[...].astype(F32) + other[...].astype(F32)).astype(BF16)
+
+    def stage(self, m, stage):
+        i, start, width, ka, kb, at = self.parts(m)
+        s, z, y, Z = self.s, self.z, self.y, self.Z
+        blocks, held, R0, R1A, R1B, R2A, R2B, out = self.arrays[i]
+        cols, A, B = pl.ds(start, width), pl.ds(start, ka), pl.ds(start + ka, kb)
+        half = pl.ds(at, ka)
+        if stage == 0:
+            own = self.own(m)
+            if own is not None:
+                own.start()
+        else:
+            if stage == 1 and held is not None:
+                self.own(m).wait()
+            for copy in self.copies(m, stage - 1):
+                copy.wait_recv()
+        if stage == 1:
+
+            @pl.loop(0, 4 * Z)
+            def _(t):
+                index = (t // (Z * 2), (t // 2) % Z, t % 2)
+                self.add(i, index, cols, R0.at[(*index, slice(None), cols)])
+
+        elif stage == 2:
+
+            @pl.loop(0, 2 * Z)
+            def _(t):
+                u, zz = t // Z, t % Z
+                self.add(i, (u, zz, y), A, R1A.at[u, zz, :, half])
+                if kb:
+                    self.add(i, (s, zz, u), B, R1B.at[zz, u, :, half])
+
+        elif stage == 3:
+
+            @pl.loop(0, Z)
+            def _(zz):
+                self.add(i, (s, zz, y), A, R2A.at[zz, :, half])
+                if kb:
+                    self.add(i, (s, zz, y), B, R2B.at[zz, :, half])
+
+        elif stage == 4:
+            out[0, :, cols] = self.held(i, (s, z, y), cols)[...]
+            return
+        for copy in self.copies(m, stage):
+            copy.start()
+
+    @property
+    def ticks(self):
+        return len(self.chunks) + 4
+
+    def tick(self, t):
         for k in range(5):
-            if 0 <= t - k < n:
-                stages[k](t - k)
-    for copy in sends:
-        copy.wait_send()
-
-
-def scatter_all(arrays, Z):
-    n = len(arrays)
+            if 0 <= t - k < len(self.chunks):
+                self.stage(t - k, k)
+
+    def finish(self):
+        for m in range(len(self.chunks)):
+            for stage in range(4):
+                for copy in self.copies(m, stage):
+                    copy.wait_send()
+
+
+def scatter_buffers(shapes, loaded, Z, chunks):
+    refs = []
+    for (r, k), load in zip(shapes, loaded):
+        ka, kb = halves(k)
+        kb = max(kb, 128)
+        if load:
+            refs.append((2, Z, 2, r, k))
+        refs += [(2, Z, 2, r, k), (2, Z, r, ka), (Z, 2, r, kb), (Z, r, ka), (Z, r, kb)]
+    n = len(chunks)
     D = pltpu.SemaphoreType.DMA
-
-    def buffers(shape_of):
-        return [pltpu.VMEM(shape_of(*a.shape[4:]), BF16) for a in arrays]
-
-    def half(columns, k):
-        return max(halves(columns)[k], 128)
-
-    return pl.pallas_call(
-        functools.partial(scatter_kernel, n, Z),
-        out_shape=[jax.ShapeDtypeStruct((Z,) + a.shape[4:], BF16) for a in arrays],
-        in_specs=[pl.BlockSpec(memory_space=pl.ANY)] * n,
-        out_specs=[pl.BlockSpec(memory_space=pltpu.VMEM)] * n,
-        scratch_shapes=buffers(lambda r, k: (2, Z, 2, r, k))
-        + buffers(lambda r, k: (2, Z, 2, r, k))
-        + buffers(lambda r, k: (2, Z, r, half(k, 0)))
-        + buffers(lambda r, k: (Z, 2, r, half(k, 1)))
-        + buffers(lambda r, k: (Z, r, half(k, 0)))
-        + buffers(lambda r, k: (Z, r, half(k, 1)))
-        + [D((n,)), D((n,)), D((n,)), D((n, 4)), D((n, 4)), D((n, Z - 1)), D((n, Z - 1))],
-        compiler_params=pltpu.CompilerParams(
-            collective_id=1, has_side_effects=True, vmem_limit_bytes=60 * 2**20
-        ),
-    )(*arrays)
+    return [pltpu.VMEM(s, BF16) for s in refs], [
+        D((n,)),
+        D((n,)),
+        D((n,)),
+        D((n, 4)),
+        D((n, 4)),
+        D((n, Z - 1)),
+        D((n, Z - 1)),
+    ]
+
+
+def take_buffers(refs, blocks, loaded, outs):
+    refs = list(refs)
+    arrays = []
+    for block, load, out in zip(blocks, loaded, outs):
+        held = refs.pop(0) if load else None
+        arrays.append((block, held, *(refs.pop(0) for _ in range(5)), out))
+    return arrays
 
 
 def nn(a, b): return jnp.dot(a, b, preferred_element_type=F32)
@@ -394,77 +445,6 @@
         scratch_shapes=[pltpu.VMEM(w.shape, BF16) for w in (qkv, proj, fc1, fc2)] + [D((4,))],
         compiler_params=params())(info, places, patches, gains, bias, qkv, proj, fc1, fc2)
 
-def enc_bwd_kernel(info, places, encoded, gemb, embed, gains, x_r, m_r, o_r, x1_r, u_r, dg_r, p_r, qkv_h, proj_h, fc1_h, fc2_h,
-                   gp_o, gembed_o, gqkv_o, gproj_o, gfc1_o, gfc2_o, gvec_o, gbias_o,
-                   qkv, proj, fc1, fc2, sfc2, sfc1, sproj, sqkv, sem):
-    copies = [pltpu.make_async_copy(h, v, sem.at[i]) for i, (h, v) in enumerate(((fc2_h, fc2), (fc1_h, fc1), (proj_h, proj), (qkv_h, qkv)))]
-    for cp in copies: cp.start()
-    ge = gemb[...]
-    gembed_o[...] = tn(encoded[...], ge).astype(BF16)
-    gy = nt(ge, embed[...]).astype(BF16)
-    G = gy.astype(F32)
-    u = u_r[...]
-    sfc2[...] = tn(u, gy).astype(BF16)
-    w2 = pltpu.make_async_copy(sfc2, gfc2_o, sem.at[4]); w2.start()
-    copies[0].wait()
-    gz = (nt(gy, fc2[...]) * dg_r[...]).astype(BF16)
-    gbias_o[...] = col_sum(gz.astype(F32))
-    x1 = x1_r[...]
-    hat2, r2 = norm_parts(x1)
-    h2 = (hat2 * (1.0 + gains[2:3]) + gains[3:4]).astype(BF16)
-    sfc1[...] = tn(h2, gz).astype(BF16)
-    w1 = pltpu.make_async_copy(sfc1, gfc1_o, sem.at[5]); w1.start()
-    copies[1].wait()
-    gh2 = nt(gz, fc1[...])
-    gvec_o[2:3, :] = col_sum(gh2 * hat2)
-    gvec_o[3:4, :] = col_sum(gh2)
-    gx1 = G + norm_back(gh2, hat2, r2, gains[2:3])
-    ga = gx1.astype(BF16)
-    gvec_o[6:7, :] = col_sum(ga.astype(F32))
-    gvec_o[7:8, :] = col_sum(G)
-    o = o_r[...]
-    sproj[...] = tn(o, ga).astype(BF16)
-    wp = pltpu.make_async_copy(sproj, gproj_o, sem.at[6]); wp.start()
-    copies[2].wait()
-    go = nt(ga, proj[...]).astype(BF16)
-    W = x1.shape[1]
-    hs = W // HEADS_E
-    gq, gk, gv = [], [], []
-    for j in range(HEADS_E):
-        q = m_r[:, hs*j:hs*(j+1)]; k = m_r[:, W+hs*j:W+hs*(j+1)]; val = m_r[:, 2*W+hs*j:2*W+hs*(j+1)]
-        g = go[:, hs*j:hs*(j+1)]
-        p = p_r[j]
-        gv.append(tn(p.astype(BF16), g).astype(BF16))
-        gp = nt(g, val)
-        gs = (p * (gp - jnp.sum(gp * p, axis=-1, keepdims=True))).astype(BF16)
-        gq.append((nn(gs, k) * hs**-0.5).astype(BF16))
-        gk.append((tn(gs, q) * hs**-0.5).astype(BF16))
-    gm = jnp.concatenate(gq + gk + gv, 1)
-    gvec_o[4:5, :] = col_sum(gm[:, :W].astype(F32))
-    gvec_o[5:6, :] = col_sum(gm[:, 2*W:].astype(F32))
-    x = x_r[...]
-    hat, r = norm_parts(x)
-    h = (hat * (1.0 + gains[0:1]) + gains[1:2]).astype(BF16)
-    sqkv[...] = tn(h, gm).astype(BF16)
-    wq = pltpu.make_async_copy(sqkv, gqkv_o, sem.at[7]); wq.start()
-    copies[3].wait()
-    gh = nt(gm, qkv[...])
-    gvec_o[0:1, :] = col_sum(gh * hat)
-    gvec_o[1:2, :] = col_sum(gh)
-    gx = gx1 + norm_back(gh, hat, r, gains[0:1])
-    pick = pick_matrix(places[...], info[0] // 10, gp_o.shape[0]).astype(F32)
-    gp_o[...] = jnp.dot(pick, gx, preferred_element_type=F32, precision=lax.Precision.HIGHEST)
-    for cp in (w2, w1, wp, wq): cp.wait()
-
-def enc_bwd(info, places, encoded, gemb, embed, gains, x, m, o, x1, u, dg, p, qkv, proj, fc1, fc2, slots):
-    W, Fw = fc1.shape
-    sd = jax.ShapeDtypeStruct
-    return pl.pallas_call(enc_bwd_kernel,
-        out_shape=(sd((slots, W), F32), sd(embed.shape, BF16), sd(qkv.shape, BF16), sd(proj.shape, BF16), sd(fc1.shape, BF16), sd(fc2.shape, BF16), sd((8, W), F32), sd((1, Fw), F32)),
-        in_specs=[S] + [V]*12 + [A]*4, out_specs=(V, V, A, A, A, A, V, V),
-        scratch_shapes=[pltpu.VMEM(w.shape, BF16) for w in (qkv, proj, fc1, fc2, fc2, fc1, proj, qkv)] + [D((8,))],
-        compiler_params=params())(info, places, encoded, gemb, embed, gains, x, m, o, x1, u, dg, p, qkv, proj, fc1, fc2)
-
 def dec_pre_kernel(info, places, encoded, embed, gains, posT, qkv, x_o, q_o, k_o, v_o):
     n = x_o.shape[0]
     i = pl.program_id(0)
@@ -533,38 +513,6 @@
         out_shape=(jax.ShapeDtypeStruct((n, W), BF16), jax.ShapeDtypeStruct((W//GROUP, 4, n), F32)),
         in_specs=[S, blk, blk, blk], out_specs=(blk, pl.BlockSpec((1, 4, n), lambda g: (g, 0, 0))),
         compiler_params=params())(info, q, k, v)
-
-def attend_back_kernel(info, q_ref, k_ref, v_ref, go_ref, o_ref, L_ref, gq_ref, gk_ref, gv_ref):
-    q = q_ref[...]; k = k_ref[...]; v = v_ref[...]; go = go_ref[...]
-    bias = dead_bias(info[0], k.shape[0])
-    qT = q.T; kT = k.T; goT = go.T; oT = o_ref[...].T
-    inner_all = goT.astype(F32) * oT.astype(F32)
-    ak = av = None
-    gqs = []
-    for j in range(4):
-        rows = slice(HD*j, HD*(j+1))
-        s = nn(k, head_rows(qT, j))
-        s = jnp.concatenate([s[:SHORT], s[SHORT:] + bias], 0)
-        p = jnp.exp2(s - L_ref[0, j:j+1, :])
-        gp = nn(v, head_rows(goT, j))
-        inner = jnp.sum(inner_all[rows], axis=0, keepdims=True)
-        gs = (p * (gp - inner)).astype(BF16)
-        a = nn(p.astype(BF16), head_lanes(go, j))
-        b = nn(gs, head_lanes(q, j))
-        av = a if av is None else av + a
-        ak = b if ak is None else ak + b
-        gqs.append((nn(kT[rows], gs) * math.log(2.0)).astype(BF16))
-    gq_ref[...] = jnp.concatenate(gqs, 0).T
-    gk_ref[...] = (ak * HD**-0.5).astype(BF16)
-    gv_ref[...] = av.astype(BF16)
-
-def attend_back(info, q, k, v, go, o, L):
-    n, W = k.shape
-    blk = pl.BlockSpec((n, GROUP), lambda g: (0, g))
-    return pl.pallas_call(attend_back_kernel, grid=(W//GROUP,),
-        out_shape=(jax.ShapeDtypeStruct((n, W), BF16),)*3,
-        in_specs=[S, blk, blk, blk, blk, blk, pl.BlockSpec((1, 4, n), lambda g: (g, 0, 0))], out_specs=(blk,)*3,
-        compiler_params=params())(info, q, k, v, go, o, L)
 
 def dec_mid_kernel(steps, info, x_r, o_r, cot_r, gains, bias, proj, fc1, fc2,
                    dec_o, gx1_o, go_o, gfc2_o, gfc1_o, gproj_o, gvec_o, gbias_o, afc2, afc1, aproj):
@@ -661,23 +609,179 @@
         scratch_shapes=[pltpu.VMEM(qkv.shape, F32), pltpu.VMEM((ROWS_E, W), F32)],
         compiler_params=params())(info, places, x, gx1, gq, gk, gv, gains, qkv)
 
-
-def unpack_kernel(small, e_gains, e_bias, d_gains, d_bias):
-    count = small.shape[0]
-    values = small[...].astype(F32)
-    for out, row, rows in ((e_gains, 0, 8), (d_gains, 8, 16), (e_bias, 24, 1), (d_bias, 25, 1)):
-        w = out.shape[1] // count
-        out[...] = jnp.concatenate([values[i, row : row + rows, :w] for i in range(count)], 1)
-
-
-def unpack(small, shapes):
+SPOTS = (0, 1, 3, 5, 7, 9, 11, 13, 15)
+
+
+def attend_back_kernel(Z, chunks, info, q_ref, k_ref, v_ref, go_ref, o_ref, L_ref, *refs):
+    blocks, (gq_ref, gk_ref, gv_ref), outs, rest = refs[:3], refs[3:6], refs[6:9], refs[9:]
+    lands, rest = rest[:3], rest[3:]
+    engine = Scatter(Z, take_buffers(rest[:-7], blocks, (True,) * 3, lands), chunks, rest[-7:])
+    g = pl.program_id(0)
+
+    @pl.when(g == 0)
+    def _():
+        engine.greet()
+
+    q = q_ref[...]
+    k = k_ref[...]
+    v = v_ref[...]
+    go = go_ref[...]
+    bias = dead_bias(info[0], k.shape[0])
+    qT, kT, goT, oT = q.T, k.T, go.T, o_ref[...].T
+    inner_all = goT.astype(F32) * oT.astype(F32)
+    ak = av = None
+    gqs = []
+    for j in range(4):
+        for step in range(4):
+            if 4 * step + j in SPOTS:
+
+                @pl.when(g == step)
+                def _():
+                    engine.tick(SPOTS.index(4 * step + j))
+
+        rows = slice(HD * j, HD * (j + 1))
+        s = nn(k, head_rows(qT, j))
+        s = jnp.concatenate([s[:SHORT], s[SHORT:] + bias], 0)
+        p = jnp.exp2(s - L_ref[0, j : j + 1, :])
+        gp = nn(v, head_rows(goT, j))
+        inner = jnp.sum(inner_all[rows], axis=0, keepdims=True)
+        gs = (p * (gp - inner)).astype(BF16)
+        a = nn(p.astype(BF16), head_lanes(go, j))
+        b = nn(gs, head_lanes(q, j))
+        av = a if av is None else av + a
+        ak = b if ak is None else ak + b
+        gqs.append((nn(kT[rows], gs) * math.log(2.0)).astype(BF16))
+    gq_ref[...] = jnp.concatenate(gqs, 0).T
+    gk_ref[...] = (ak * HD**-0.5).astype(BF16)
+    gv_ref[...] = av.astype(BF16)
+
+    @pl.when(g == 3)
+    def _():
+        engine.finish()
+        for out, land in zip(outs, lands):
+            out[...] = land[...]
+
+
+def attend_back(info, q, k, v, go, o, L, grads, Z):
+    n, W = k.shape
+    blk = pl.BlockSpec((n, GROUP), lambda g: (0, g))
+    shapes = [a.shape[4:] for a in grads]
+    chunks = []
+    for i, (r, c) in enumerate(shapes[:2]):
+        chunks += [(i, 0, c // 2), (i, c // 2, c // 2)]
+    chunks.append((2, 0, shapes[2][1]))
+    buffers, sems = scatter_buffers(shapes, (True,) * 3, Z, chunks)
+    outs = [jax.ShapeDtypeStruct((Z, *s), BF16) for s in shapes]
     return pl.pallas_call(
-        unpack_kernel, out_shape=[jax.ShapeDtypeStruct(s, F32) for s in shapes]
-    )(small)
-
-
-def pack_kernel(e_vec, e_bias, mid_vec, post_vec, d_bias, out, whole):
-    count = out.shape[0]
+        functools.partial(attend_back_kernel, Z, chunks),
+        grid=(W // GROUP,),
+        out_shape=[jax.ShapeDtypeStruct((n, W), BF16)] * 3 + outs,
+        in_specs=[S, blk, blk, blk, blk, blk, pl.BlockSpec((1, 4, n), lambda g: (g, 0, 0))]
+        + [A] * 3,
+        out_specs=[blk] * 3 + [V] * 3,
+        scratch_shapes=[pltpu.VMEM(a.shape, BF16) for a in outs] + buffers + sems,
+        compiler_params=pltpu.CompilerParams(
+            collective_id=1, has_side_effects=True, vmem_limit_bytes=60 * 2**20
+        ),
+    )(info, q, k, v, go, o, L, *grads)
+
+
+def enc_bwd_kernel(Z, chunks, *refs):
+    given, small_in, blocks_in = refs[:14], refs[14:18], refs[18:20]
+    gx_o, outs, rest = refs[20], refs[21:29], refs[29:]
+    local, made, rest = rest[:13], rest[13:19], rest[19:]
+    e_vec, e_bias, whole, sem = rest[-11:-7]
+    loaded = (True, True) + (False,) * 6
+    engine = Scatter(
+        Z, take_buffers(rest[:-11], (*blocks_in, *made), loaded, outs), chunks, rest[-7:]
+    )
+    g_embed, g_fc2, g_fc1, g_proj, g_qkv, g_small = made
+    gains, mid_vec, post_vec, d_bias = small_in
+    places = (*local, local[8].at[:, pl.ds(0, given[13].shape[1])])
+    loads = [pltpu.make_async_copy(given[i], places[i], sem.at[i]) for i in range(14)]
+    for load in loads[:13]:
+        load.start()
+
+    def got(i):
+        loads[i].wait()
+        return places[i][...]
+
+    engine.greet()
+    steps = iter(range(engine.ticks))
+
+    def tick():
+        engine.tick(next(steps))
+
+    def store(ref, value):
+        ref[...] = value.astype(BF16).reshape(ref.shape)
+
+    tick()
+    ge = got(0)
+    store(g_embed, tn(got(1), ge))
+    gy = nt(ge, got(2)).astype(BF16)
+    G = gy.astype(F32)
+    tick()
+    u = got(3)
+    store(g_fc2, tn(u, gy))
+    tick()
+    gz = (nt(gy, got(4)) * got(5)).astype(BF16)
+    e_bias[...] = col_sum(gz.astype(F32))
+    tick()
+    hat2, r2 = norm_parts(got(6))
+    h2 = (hat2 * (1.0 + gains[2:3]) + gains[3:4]).astype(BF16)
+    store(g_fc1, tn(h2, gz))
+    tick()
+    gh2 = nt(gz, got(8))
+    loads[13].start()
+    e_vec[2:3, :] = col_sum(gh2 * hat2)
+    e_vec[3:4, :] = col_sum(gh2)
+    gx1 = G + norm_back(gh2, hat2, r2, gains[2:3])
+    ga = gx1.astype(BF16)
+    e_vec[6:7, :] = col_sum(ga.astype(F32))
+    e_vec[7:8, :] = col_sum(G)
+    store(g_proj, tn(got(7), ga))
+    tick()
+    go = nt(ga, got(9)).astype(BF16)
+    for i in (10, 11, 12):
+        loads[i].wait()
+    m_r, p_r, x_r = places[10:13]
+    W = gx1.shape[1]
+    hs = W // HEADS_E
+    gq, gk, gv = [], [], []
+    for j in range(HEADS_E):
+        q = m_r[:, hs * j : hs * (j + 1)]
+        k = m_r[:, W + hs * j : W + hs * (j + 1)]
+        val = m_r[:, 2 * W + hs * j : 2 * W + hs * (j + 1)]
+        g = go[:, hs * j : hs * (j + 1)]
+        p = p_r[j]
+        gv.append(tn(p.astype(BF16), g).astype(BF16))
+        gp = nt(g, val)
+        gs = (p * (gp - jnp.sum(gp * p, axis=-1, keepdims=True))).astype(BF16)
+        gq.append((nn(gs, k) * hs**-0.5).astype(BF16))
+        gk.append((tn(gs, q) * hs**-0.5).astype(BF16))
+        if j == HEADS_E // 2:
+            tick()
+    gm = jnp.concatenate(gq + gk + gv, 1)
+    tick()
+    e_vec[4:5, :] = col_sum(gm[:, :W].astype(F32))
+    e_vec[5:6, :] = col_sum(gm[:, 2 * W :].astype(F32))
+    hat, r = norm_parts(x_r[...])
+    h = (hat * (1.0 + gains[0:1]) + gains[1:2]).astype(BF16)
+    store(g_qkv, tn(h, gm))
+    tick()
+    gh = nt(gm, got(13))
+    e_vec[0:1, :] = col_sum(gh * hat)
+    e_vec[1:2, :] = col_sum(gh)
+    gx_o[...] = gx1 + norm_back(gh, hat, r, gains[0:1])
+    pack(g_small, e_vec, e_bias, mid_vec, post_vec, d_bias, whole)
+    for t in steps:
+        engine.tick(t)
+    engine.finish()
+
+
+def pack(out, e_vec, e_bias, mid_vec, post_vec, d_bias, whole):
+    Z = out.shape[1]
+    count = 8 * Z
     whole[...] = jnp.zeros_like(whole)
     whole[0:2] = post_vec[0:2]
     whole[2:4] = mid_vec[0:2]
@@ -689,19 +793,66 @@
         w = ref.shape[1] // count
         values = ref[...].astype(BF16)
         for i in range(count):
-            out[i, row : row + rows, :w] = values[:, w * i : w * i + w]
-
-
-def pack(e_vec, e_bias, mid_vec, post_vec, d_bias, count):
+            at = (i // (4 * Z), i // 4 % Z, i // 2 % 2, i % 2)
+            out[(*at, slice(row, row + rows), slice(0, w))] = values[:, w * i : w * i + w]
+
+
+def enc_bwd(encoded, gemb, embed, kept, mats, small_in, blocks_in, Z):
+    x, m, o, x1, u, dg, p = kept
+    qkv, proj, fc1, fc2 = mats
+    given = (gemb, encoded, embed, u, fc2, dg, x1, o, fc1, proj, m, p, x, qkv)
+    count = 8 * Z
+
+    def block_shape(a):
+        return (a.shape[0] // count, a.shape[1])
+
+    shapes = [a.shape[4:] for a in blocks_in]
+    shapes += [block_shape(a) for a in (embed, fc2, fc1, proj, qkv)] + [(SMALL_ROWS, 128)]
+    W, Fw = fc1.shape
+    chunks = [(0, 0, shapes[0][1]), (1, 0, shapes[1][1]), (2, 0, shapes[2][1])]
+    chunks += [(3, t * W // 3, W // 3) for t in range(3)]
+    chunks += [(4, t * Fw // 3, Fw // 3) for t in range(3)]
+    chunks += [(5, 0, W)] + [(6, t * W, W) for t in range(3)] + [(7, 0, 128)]
+    loaded = (True, True) + (False,) * 6
+    buffers, sems = scatter_buffers(shapes, loaded, Z, chunks)
+    sd = jax.ShapeDtypeStruct
     return pl.pallas_call(
-        pack_kernel,
-        out_shape=jax.ShapeDtypeStruct((count, SMALL_ROWS, 128), BF16),
-        scratch_shapes=[pltpu.VMEM((16, mid_vec.shape[1]), F32)],
-    )(e_vec, e_bias, mid_vec, post_vec, d_bias)
-
-
-def last_kernel(n, *refs):
-    ins, outs = refs[:n], refs[n:]
+        functools.partial(enc_bwd_kernel, Z, chunks),
+        out_shape=[sd(x.shape, F32)] + [sd((Z, *s), BF16) for s in shapes],
+        in_specs=[A] * 14 + [V] * 4 + [A] * 2,
+        out_specs=[V] * 9,
+        scratch_shapes=[pltpu.VMEM(a.shape, a.dtype) for a in given[:13]]
+        + [pltpu.VMEM((2, Z, 2, 2, *s), BF16) for s in shapes[2:]]
+        + buffers
+        + [pltpu.VMEM((8, W), F32), pltpu.VMEM((1, Fw), F32), pltpu.VMEM((16, embed.shape[1]), F32)]
+        + [D((14,))]
+        + sems,
+        compiler_params=pltpu.CompilerParams(
+            collective_id=2, has_side_effects=True, vmem_limit_bytes=62 * 2**20
+        ),
+    )(*given, *small_in, *blocks_in)
+
+
+def unpack_kernel(small, e_gains, e_bias, d_gains, d_bias):
+    count = small.shape[0]
+    values = small[...].astype(F32)
+    for out, row, rows in ((e_gains, 0, 8), (d_gains, 8, 16), (e_bias, 24, 1), (d_bias, 25, 1)):
+        w = out.shape[1] // count
+        out[...] = jnp.concatenate([values[i, row : row + rows, :w] for i in range(count)], 1)
+
+
+def unpack(small, shapes):
+    return pl.pallas_call(
+        unpack_kernel, out_shape=[jax.ShapeDtypeStruct(s, F32) for s in shapes]
+    )(small)
+
+
+def last_kernel(n, info, places, gx, *refs):
+    ins, g_patch, outs = refs[:n], refs[n], refs[n + 1 :]
+    pick = pick_matrix(places[...], info[0] // 10, g_patch.shape[0]).astype(F32)
+    g_patch[...] = jnp.dot(
+        pick, gx[...], preferred_element_type=F32, precision=lax.Precision.HIGHEST
+    )
 
     def total(ref):
         acc = ref[0].astype(F32)
@@ -716,12 +867,13 @@
         outs[4 + i][...] = total(ref).T if i == POS_AT else total(ref)
 
 
-def last_sums(arrays, shapes):
+def last_sums(info, places, gx, arrays, shapes):
     return pl.pallas_call(
         functools.partial(last_kernel, len(arrays)),
         out_shape=[jax.ShapeDtypeStruct(s, F32) for s in shapes],
+        in_specs=[S] + [V] * (2 + len(arrays)),
         compiler_params=params(),
-    )(*arrays)
+    )(info, places, gx, *arrays)
 
 
 def body(
@@ -773,22 +925,30 @@
     decoded, gx1, go, gd_fc2, gd_fc1, gd_proj, mid_vec, gd_bias = dec_mid(
         info, x, o, cotangent[0], d_gains, d_bias, dw_proj, dw_fc1, dw_fc2
     )
-    gq, gk, gv = attend_back(info, q, k, v, go, o, L)
+
+    def blocks(m):
+        return m.reshape((2, Z, 2, 2, -1, m.shape[-1]))
+
+    gq, gk, gv, *early = attend_back(
+        info, q, k, v, go, o, L, [blocks(m) for m in (gd_fc2, gd_fc1, gd_proj)], Z
+    )
     gd_qkv, g_posT, gemb, post_vec = dec_post(
         info, places, x, gx1, gq, gk, gv, d_gains, dw_qkv
     )
-    g_patch, g_embed, ge_qkv, ge_proj, ge_fc1, ge_fc2, e_vec, ge_bias = enc_bwd(
-        info, places, encoded, gemb, w_embed, e_gains, *kept, w_qkv, w_proj, w_fc1, w_fc2, slots
-    )
-    g_small = pack(e_vec, ge_bias, mid_vec, post_vec, gd_bias, count)
-
-    def blocks(m):
-        return m.reshape((2, Z, 2, 2, -1, m.shape[-1]))
-
-    order = (gd_fc2, gd_fc1, gd_proj, gd_qkv, g_posT, g_embed, ge_fc2, ge_fc1, ge_proj, ge_qkv)
-    parts = scatter_all([blocks(m) for m in order + (g_small.reshape(-1, 128),)], Z)
-    shapes = [m.shape for m in smalls + shards]
-    out = last_sums(parts[::-1], shapes)
+    gx, *late = enc_bwd(
+        encoded,
+        gemb,
+        w_embed,
+        kept,
+        (w_qkv, w_proj, w_fc1, w_fc2),
+        (e_gains, mid_vec, post_vec, gd_bias),
+        (blocks(gd_qkv), blocks(g_posT)),
+        Z,
+    )
+    pd_qkv, p_pos, p_embed, p_fc2, p_fc1, p_proj, p_qkv, p_small = late
+    parts = (p_small, p_qkv, p_proj, p_fc1, p_fc2, p_embed, p_pos, pd_qkv, *early[::-1])
+    shapes = [(slots, patches.shape[2])] + [m.shape for m in smalls + shards]
+    g_patch, *out = last_sums(info, places, gx, parts, shapes)
     re_vec, rd_vec, re_bias, rd_bias = out[:4]
     re_qkv, re_proj, re_fc1, re_fc2, r_embed, r_pos, rd_qkv, rd_proj, rd_fc1, rd_fc2 = out[4:]
     return (

time: 417 us -> 383 us (0.918)
  Pallas kernels: 404 us -> 370 us
    pallas_call x4 -> x2, Pallas kernels: 189 us -> 152 us  [the longest x1 94.3 us: enc_bwd(): pl.pallas_call(functools.partial(enc_bwd_kernel, Z, chunks), out_shape=[s...]
where the time goes in v3:
time: 383 us; the launch traced here: 377 us
  Pallas kernels  370 us (97%)
  local copies, waits for them, and re-layouts  5.52 us (1%)
    pallas_call x1, Pallas kernels, gather_all(): pl.pallas_call(functools.partial(gather_kernel, n, Z), out_shape=[jax.Sha...  118 us
    pallas_call x1, Pallas kernels, enc_bwd(): pl.pallas_call(functools.partial(enc_bwd_kernel, Z, chunks), out_shape=[s...  94.3 us
    pallas_call x1, Pallas kernels, attend_back(): pl.pallas_call(functools.partial(attend_back_kernel, Z, chunks), grid=(W...  57.6 us
    pallas_call x1, Pallas kernels, dec_mid(): pl.pallas_call(functools.partial(dec_mid_kernel, n // tile), grid=(n // t...  31.8 us
    pallas_call x1, Pallas kernels, attend(): pl.pallas_call(attend_kernel, grid=(W // GROUP,), out_shape=(jax.ShapeDty...  26 us
    pallas_call x1, Pallas kernels, enc_fwd(): pl.pallas_call(enc_fwd_kernel, out_shape=(sd((ROWS_E, W), BF16), sd((ROWS...  13.4 us
    pallas_call x1, Pallas kernels, dec_post(): pl.pallas_call(functools.partial(dec_post_kernel, n // tile), grid=(n //...  11.6 us
    pallas_call x1, Pallas kernels, dec_pre(): pl.pallas_call(dec_pre_kernel, grid=(n // tile,), out_shape=(sd((n, W), F...  8.62 us

profile of v3, /device:TPU:0, one launch (start us, length us, event | category | flops | bytes accessed | tf_op | source)
XLA Modules:
  0.0 376.6 jit_solution(14967936556169775303)
XLA Ops:
  0.6 0.0 copy-start
  0.7 1.3 dynamic_slice.6.info
  2.0 0.0 copy-done
  2.0 0.5 constant_dynamic-slice_fusion.places
  2.5 1.8 copy.34.refs_9_
  4.3 117.9 %shard_map.297 = (bf16[2,4,2,2,32,128]{5,4,3,2,1,0:T(8,128)(2,1)}, bf16[2,4,2,2,24,2304]{5,4,3,2,1,0:T(8,128)(2,1)}, bf16[2,4,2,2,24,768]{5,4,3,2,1,0:T(8,128)(2...) custom-call(f32[8,24]{1,0:T(8,128)} %refs_0_.1, ...), custom_call_target="tpu_custom_call" | custom-call | tf_op jit(solution)/shard_map/pallas_call | solution.py:160
  122.2 1.7 shard_map.298
  123.9 13.4 %shard_map.299 = (bf16[128,768]{1,0:T(8,128)(2,1)}, f32[128,768]{1,0:T(8,128)}, bf16[128,2304]{1,0:T(8,128)(2,1)}, bf16[128,768]{1,0:T(8,128)(2,1)}, f32[128,768...) custom-call(s32[1]{0:T(128)} %dynamic_slice.6.info, ...), custom_call_target="tpu_custom_call" | custom-call | tf_op jit(solution)/shard_map/pallas_call | solution.py:441
  137.3 8.6 %shard_map.300 = (f32[1024,512]{1,0:T(8,128)}, bf16[1024,512]{1,0:T(8,128)(2,1)}, bf16[1024,512]{1,0:T(8,128)(2,1)}, bf16[1024,512]{1,0:T(8,128)(2,1)}) custom-call(s32[1]{0:T(128)} %dynamic_slice.6.info, s32[1,128]{1,0:T(1,128)} %constant_dynamic-slice_fusion.places, bf16[128,768]{1,0:T(8,128)(2,1)} %get-tuple-element.94.encoded.refs_1_, ...), custom_call_target="tpu_custom_call" | custom-call | tf_op jit(solution)/shard_map/pallas_call | solution.py:472
  146.0 26.0 %shard_map.301 = (bf16[1024,512]{1,0:T(8,128)(2,1)}, f32[4,4,1024]{2,1,0:T(4,128)}) custom-call(s32[1]{0:T(128)} %dynamic_slice.6.info, bf16[1024,512]{1,0:T(8,128)(2,1)} %get-tuple-element.100.q_ref, bf16[1024,512]{1,0:T(8,128)(2,1)} %get-tuple-element.101.k_ref, bf16[1024,512]{1,0:T(8,128)(2,1)} %get-tuple-element.102.v_ref), custom_call_target="tpu_custom_call" | custom-call | tf_op jit(solution)/shard_map/pallas_call | solution.py:512
  171.9 31.8 %shard_map.302 = (bf16[1024,512]{1,0:T(8,128)(2,1)}, f32[1024,512]{1,0:T(8,128)}, bf16[1024,512]{1,0:T(8,128)(2,1)}, bf16[2048,512]{1,0:T(8,128)(2,1)}, bf16[512...) custom-call(s32[1]{0:T(128)} %dynamic_slice.6.info, ...), custom_call_target="tpu_custom_call" | custom-call | tf_op jit(solution)/shard_map/pallas_call | solution.py:562
  203.7 57.6 %shard_map.303 = (bf16[1024,512]{1,0:T(8,128)(2,1)}, bf16[1024,512]{1,0:T(8,128)(2,1)}, bf16[1024,512]{1,0:T(8,128)(2,1)}, bf16[4,64,512]{2,1,0:T(8,128)(2,1)}, ...) custom-call(s32[1]{0:T(128)} %dynamic_slice.6.info, bf16[1024,512]{1,0:T(8,128)(2,1)} %get-tuple-element.100.q_ref, ...), custom_call_target="tpu_custom_call" | custom-call | tf_op jit(solution)/shard_map/pallas_call | solution.py:675
  261.3 11.6 %shard_map.304 = (bf16[512,1536]{1,0:T(8,128)(2,1)}, bf16[512,1024]{1,0:T(8,128)(2,1)}, bf16[128,512]{1,0:T(8,128)(2,1)}, f32[16,512]{1,0:T(8,128)}) custom-call(s32[1]{0:T(128)} %dynamic_slice.6.info, s32[1,128]{1,0:T(1,128)} %constant_dynamic-slice_fusion.places, f32[1024,512]{1,0:T(8,128)} %get-tuple-element.99.x_r, ...), custom_call_target="tpu_custom_call" | custom-call | tf_op jit(solution)/shard_map/pallas_call | solution.py:606
  272.9 94.3 %shard_map.305 = (f32[128,768]{1,0:T(8,128)}, bf16[4,16,1536]{2,1,0:T(8,128)(2,1)}, bf16[4,16,1024]{2,1,0:T(8,128)(2,1)}, bf16[4,24,512]{2,1,0:T(8,128)(2,1)}, b...) custom-call(bf16[128,512]{1,0:T(8,128)(2,1)} %get-tuple-element.118., ...), custom_call_target="tpu_custom_call" | custom-call | tf_op jit(solution)/shard_map/pallas_call | solution.py:819
  367.2 7.3 %shard_map.306 = (f32[1024,768]{1,0:T(8,128)}, f32[8,24]{1,0:T(8,128)}, f32[10,16]{1,0:T(8,128)}, f32[1,96]{1,0:T(1,128)}, f32[1,64]{1,0:T(1,128)}, /*index=5*/f...) custom-call(s32[1]{0:T(128)} %dynamic_slice.6.info, ...), custom_call_target="tpu_custom_call" | custom-call | tf_op jit(solution)/shard_map/pallas_call | solution.py:871
  374.6 1.8 copy.35
Async XLA Ops:
  0.6 1.3 copy-start
